TPU v7x, 128 devices: a whole 4x4x4 slice. The times are simulated.
128 devices in a mesh: ctx: 8 (over y, x_hi), tp: 16 (over x_lo, z, core).
Axes of the slice: x: 4 (x_hi: 2, x_lo: 2; x = x_hi * 2 + x_lo), y: 4, z: 4, core: 2. Of those that a mesh axis runs over, the one named last changes fastest.
Arguments:
- hidden: bfloat16 [2048, 53248], P('ctx', 'tp'), may hold values from -6 to 6
- sign_bits: int32 [53248], P('tp'), may hold values from 0 to 1
- weight_codes: int32 [53248, 8192], P('tp', 'ctx'), may hold values from 0 to 15
- weight_exps: int32 [1664, 8192], P('tp', 'ctx'), may hold values from 0 to 3
Outputs:
- projected: float32 [2048, 8192], P('tp', 'ctx')
All inputs are finite; a program needn't handle non-finite values.
Results may differ from a plain program's by a relative error of at most 0.0029.
Values may be sent and summed in bfloat16 or wider, within the bound.
No kernel may reach another device: no remote copies, remote signals or barrier semaphores. Data moves between devices by JAX's collectives and lax.ppermute only.
A program may use at most 256 MiB of HBM per device.

v0:
```python
import math

import jax
import jax.numpy as jnp
import numpy as np
from jax import lax
from jax.sharding import PartitionSpec as P


def swapped(block, axis, bit):
    count = lax.axis_size(axis)
    route = []
    for low in range(count):
        high = low | 1 << bit
        if high != low and high < count:
            route += [(low, high), (high, low)]
    return lax.ppermute(block, axis, route)


def paley_matrix():
    elements = [(first_part, second_part) for first_part in range(5) for second_part in range(5)]
    squares = set()
    for left_elem in elements:
        if left_elem != (0, 0):
            squares.add(
                (
                    (left_elem[0] * left_elem[0] + 3 * left_elem[1] * left_elem[1]) % 5,
                    2 * left_elem[0] * left_elem[1] % 5,
                )
            )
    jacobs = np.zeros((25, 25))
    for row_index in range(25):
        for col_index in range(25):
            left_elem = elements[row_index]
            right_elem = elements[col_index]
            differ = ((left_elem[0] - right_elem[0]) % 5, (left_elem[1] - right_elem[1]) % 5)
            if differ == (0, 0):
                jacobs[row_index, col_index] = 0.0
            elif differ in squares:
                jacobs[row_index, col_index] = 1.0
            else:
                jacobs[row_index, col_index] = -1.0
    conference = np.zeros((26, 26))
    conference[0, 1:] = 1.0
    conference[1:, 0] = 1.0
    conference[1:, 1:] = jacobs
    result = np.kron(conference, np.array([[1.0, 1.0], [1.0, -1.0]])) + np.kron(
        np.eye(26), np.array([[1.0, -1.0], [-1.0, -1.0]])
    )
    return result


def sylvester(matrix_order):
    row_ids = lax.broadcasted_iota(jnp.int32, (matrix_order, matrix_order), 0)
    col_ids = lax.broadcasted_iota(jnp.int32, (matrix_order, matrix_order), 1)
    shared = jnp.bitwise_and(row_ids, col_ids)
    parity = jnp.zeros((matrix_order, matrix_order), jnp.int32)
    for bit_index in range(matrix_order.bit_length() - 1):
        parity = jnp.bitwise_xor(parity, jnp.bitwise_and(jnp.right_shift(shared, bit_index), 1))
    return (1 - 2 * parity).astype(jnp.float32)


def decode_weights(codes, exponents):
    magnitude = jnp.bitwise_and(codes, 7).astype(jnp.float32)
    value = jnp.where(
        magnitude < 4.0,
        magnitude * 0.5,
        jnp.where(magnitude < 6.0, magnitude - 2.0, 2.0 * magnitude - 8.0),
    )
    value = jnp.where(codes >= 8, -value, value)
    scales = jnp.where(
        exponents == 0,
        2.0 ** (-11),
        jnp.where(
            exponents == 1, 2.0 ** (-10), jnp.where(exponents == 2, 2.0 ** (-9), 2.0 ** (-8))
        ),
    ).astype(jnp.float32)
    blocks = value.reshape(codes.shape[0] // 32, 32, codes.shape[1]) * scales[:, None, :]
    return blocks.reshape(codes.shape).astype(jnp.bfloat16)


def rotate(row_block, sign_local):
    count_rows = row_block.shape[0]
    row_width = row_block.shape[1]
    local_order = row_width // 52
    groups = lax.axis_size("tp")
    flips = (1 - 2 * sign_local).astype(jnp.float32)
    signed = row_block.astype(jnp.float32) * flips[None, :]
    folded = signed.reshape(count_rows, local_order, 52)
    paley = jnp.asarray(paley_matrix(), jnp.float32)
    folded = jnp.einsum("rcp,pq->rcq", folded, paley, precision=lax.Precision.HIGHEST)
    folded = jnp.einsum(
        "rcq,ce->req", folded, sylvester(local_order), precision=lax.Precision.HIGHEST
    )
    spread = folded.reshape(count_rows, row_width)
    device_rank = lax.axis_index("tp")
    for bit_index in range(groups.bit_length() - 1):
        partner = swapped(spread, "tp", bit_index)
        on_high = jnp.bitwise_and(jnp.right_shift(device_rank, bit_index), 1) == 1
        spread = jnp.where(on_high, partner - spread, spread + partner)
    scaling = 1.0 / math.sqrt(52 * local_order * groups)
    return (spread * scaling).astype(jnp.bfloat16)


def shards(hidden, sign_bits, weight_codes, weight_exps):
    moving = rotate(hidden, sign_bits)
    gathered = lax.all_gather(moving, "ctx", axis=0, tiled=True)
    weight_down = decode_weights(weight_codes, weight_exps)
    return lax.psum_scatter(
        jnp.dot(gathered, weight_down, preferred_element_type=jnp.float32),
        "tp",
        scatter_dimension=0,
        tiled=True,
    )


def solution(mesh):
    return jax.shard_map(
        shards,
        mesh=mesh,
        in_specs=(P("ctx", "tp"), P("tp"), P("tp", "ctx"), P("tp", "ctx")),
        out_specs=P("tp", "ctx"),
        check_vma=False,
    )
```

profile of v0, /device:TPU:1, one launch (start us, length us, event | category | flops | bytes accessed | tf_op | source)
XLA Modules:
  0.0 543.7 jit_solution(10751676997992306486)
XLA Ops:
  6.5 0.0 all-gather.2.cloned.1.call-start
  6.5 0.7 subtract_convert_fusion
  7.3 1.7 convert_multiply_fusion
  8.9 3.0 copy.6
  11.9 4.7 reshape.11
  16.6 0.0 copy-done.2
  16.6 5.6 %fusion.43 = f32[256,64,52]{0,2,1:T(8,128)S(1)} fusion(f32[256,64,52]{0,2,1:T(8,128)} %reshape.11, f32[52,52,1]{1,0,2:T(8,128)S(1)} %copy-done.2), kind=kOutput, calls=%fused_computation.51 | convolution fusion | flops 531628032 | bytes 6826560 | tf_op jit(solution)/shard_map/rcp,pq->rcq/dot_general | solution.py:91
  22.2 4.1 fusion.4
  26.3 3.8 copy.7
  30.0 2.9 reshape.12
  32.9 1.5 collective-permute-start
  34.4 0.2 copy-done.1
  34.6 5.6 %collective-permute-done = f32[256,3328]{0,1:T(8,128)} collective-permute-done((f32[256,3328]{0,1:T(8,128)S(1)}, f32[256,3328]{0,1:T(8,128)}, u32[]{:S(2)}, u32[]{:S(2)}) %collective-permute-start) | collective-permute-done | bytes 3407904 | tf_op jit(solution)/shard_map/ppermute | solution.py:17
  40.2 3.4 add_select_fusion.2
  43.7 0.0 copy-start
  43.7 2.0 collective-permute-start.1
  45.7 73.9 %collective-permute-done.1 = f32[256,3328]{0,1:T(8,128)} collective-permute-done((f32[256,3328]{0,1:T(8,128)S(1)}, f32[256,3328]{0,1:T(8,128)}, u32[]{:S(2)}, u32[]{:S(2)}) %collective-permute-start.1) | collective-permute-done | bytes 3407904 | tf_op jit(solution)/shard_map/ppermute | solution.py:17
  119.5 3.4 add_select_fusion.1
  123.0 3.2 collective-permute-start.2
  126.2 73.0 %collective-permute-done.2 = f32[256,3328]{0,1:T(8,128)} collective-permute-done((f32[256,3328]{0,1:T(8,128)S(1)}, f32[256,3328]{0,1:T(8,128)}, u32[]{:S(2)}, u32[]{:S(2)}) %collective-permute-start.2) | collective-permute-done | bytes 3407904 | tf_op jit(solution)/shard_map/ppermute | solution.py:17
  199.1 4.1 add_select_fusion
  203.2 1.2 collective-permute-start.3
  204.5 72.4 %collective-permute-done.3 = f32[256,3328]{0,1:T(8,128)S(1)} collective-permute-done((f32[256,3328]{0,1:T(8,128)}, f32[256,3328]{0,1:T(8,128)S(1)}, u32[]{:S(2)}, u32[]{:S(2)}) %collective-permute-start.3) | collective-permute-done | bytes 3407904 | tf_op jit(solution)/shard_map/ppermute | solution.py:17
  276.8 3.7 multiply_convert_fusion
  280.5 0.0 all-gather.2.cloned.1.call-update
  280.6 0.0 reduce-scatter.2.cloned.1.call-start
  280.6 1.1 select_select_fusion
  281.7 11.0 %fusion.1 = bf16[3328,1024]{1,0:T(8,128)(2,1)} fusion(s32[3328,1024]{1,0:T(8,128)} %param.7, f32[104,1024]{1,0:T(8,128)S(1)} %select_select_fusion), kind=kLoop, calls=%fused_computation.2 | loop fusion | flops 51118080 | bytes 20873216 | tf_op jit(solution)/shard_map/convert_element_type | solution.py:79
  292.7 154.3 %all-gather.2.cloned.1.call-done = bf16[2048,3328]{0,1:T(8,128)(2,1)} async-done(((bf16[256,3328]{0,1:T(8,128)(2,1)}), bf16[2048,3328]{0,1:T(8,128)(2,1)}) %all-gather.2.cloned.1.call-update) | async-done | bytes 13631504 | tf_op jit(solution)/shard_map/all_gather | solution.py:107
  446.9 20.1 %fusion.44 = f32[2048,1024]{1,0:T(8,128)} fusion(bf16[2048,3328]{0,1:T(8,128)(2,1)} %all-gather.2.cloned.1.call-done, bf16[3328,1024]{1,0:T(8,128)(2,1)} %fusion.1), kind=kOutput, calls=%fused_computation.52 | convolution fusion | flops 13958643712 | bytes 28835840 | tf_op jit(solution)/shard_map/dot_general | solution.py:110
  467.1 0.0 reduce-scatter.2.cloned.1.call-update
  467.1 69.7 %reduce-scatter.2.cloned.1.call-done = f32[128,1024]{1,0:T(8,128)} async-done(((f32[2048,1024]{1,0:T(8,128)}), f32[128,1024]{1,0:T(8,128)}) %reduce-scatter.2.cloned.1.call-update) | async-done | bytes 524304 | tf_op jit(solution)/shard_map/reduce_scatter | solution.py:109
  (3 shorter events, 0.0 us)
Async XLA Ops:
  6.5 440.4 %all-gather.2.cloned.1.call-start = ((), (), s32[]{:S(2)}) async-start(), calls=%async_computation.1 | async-start | bytes 15335424 | tf_op jit(solution)/shard_map/all_gather | solution.py:107
  11.9 4.7 copy-start.2
  32.9 1.7 copy-start.1
  32.9 7.3 %collective-permute-start = (f32[256,3328]{0,1:T(8,128)S(1)}, f32[256,3328]{0,1:T(8,128)}, u32[]{:S(2)}, u32[]{:S(2)}) collective-permute-start(f32[256,3328]{0,1:T(8,128)S(1)} %reshape.12), channel_id=1, source_target_pairs={{0,1},{1,0},{2,3},{3,2},{4,5},{5,4},{6,7},{7,6},{8,9},{9,8},{10,11... | collective-permute-start | bytes 10223624 | tf_op jit(solution)/shard_map/ppermute | solution.py:17
  43.7 2.0 copy-start
  43.7 75.9 %collective-permute-start.1 = (f32[256,3328]{0,1:T(8,128)S(1)}, f32[256,3328]{0,1:T(8,128)}, u32[]{:S(2)}, u32[]{:S(2)}) collective-permute-start(f32[256,3328]{0,1:T(8,128)S(1)} %add_select_fusion.2), channel_id=1, source_target_pairs={{0,2},{2,0},{1,3},{3,1},{4,6},{6,4},{5,7},{7,5},{8,10},{10,8},{9,1... | collective-permute-start | bytes 10223624 | tf_op jit(solution)/shard_map/ppermute | solution.py:17
  123.0 76.2 %collective-permute-start.2 = (f32[256,3328]{0,1:T(8,128)S(1)}, f32[256,3328]{0,1:T(8,128)}, u32[]{:S(2)}, u32[]{:S(2)}) collective-permute-start(f32[256,3328]{0,1:T(8,128)S(1)} %add_select_fusion.1), channel_id=1, source_target_pairs={{0,4},{4,0},{1,5},{5,1},{2,6},{6,2},{3,7},{7,3},{8,12},{12,8},{9,1... | collective-permute-start | bytes 10223624 | tf_op jit(solution)/shard_map/ppermute | solution.py:17
  203.2 73.6 %collective-permute-start.3 = (f32[256,3328]{0,1:T(8,128)}, f32[256,3328]{0,1:T(8,128)S(1)}, u32[]{:S(2)}, u32[]{:S(2)}) collective-permute-start(f32[256,3328]{0,1:T(8,128)} %add_select_fusion), channel_id=1, source_target_pairs={{0,8},{8,0},{1,9},{9,1},{2,10},{10,2},{3,11},{11,3},{4,12},{12,4},... | collective-permute-start | bytes 10223624 | tf_op jit(solution)/shard_map/ppermute | solution.py:17
  280.6 256.3 %reduce-scatter.2.cloned.1.call-start = ((), (), s32[]{:S(2)}) async-start(), calls=%async_computation.2 | async-start | bytes 8912896 | tf_op jit(solution)/shard_map/reduce_scatter | solution.py:109
Sparse Core Ops, SparseCore 0:
  280.7 166.2 all-gather.1
  467.2 69.5 reduce-scatter.1
where the time goes:
time: 547 us; the launch traced here: 544 us
  waiting for transfers between devices  449 us (82%)
  matrix products  29.8 us (5%)
  other arithmetic  29.1 us (5%)
  local copies, waits for them, and re-layouts  14.5 us (3%)
  between operations  13.5 us (2%)
  starting transfers between devices  7.94 us (1%)
    ppermute x4, waiting for transfers between devices, swapped(): return lax.ppermute(block, axis, route)  225 us
    all_gather x1, waiting for transfers between devices, shards(): gathered = lax.all_gather(moving, 'ctx', axis=0, tiled=True)  154 us
    reduce_scatter x1, waiting for transfers between devices, shards(): lax.psum_scatter(jnp.dot(gathered, weight_down, preferred_element_type=jn...  69.7 us
    dot_general x1, matrix products, shards(): jnp.dot(gathered, weight_down, preferred_element_type=jnp.float32)  20.1 us
    select_n x3, other arithmetic, rotate(): spread = jnp.where(on_high, partner - spread, spread + partner)  11 us
    convert_element_type x1, other arithmetic, decode_weights(): return blocks.reshape(codes.shape).astype(jnp.bfloat16)  11 us
  transfers between devices with their start and end apart: 6, of which 6 were waited for; matrix products, arithmetic and copies ran while one was open for 2% of the time, Pallas kernels for 0%

commit v1 on v0

v1 whole, which is shorter than its diff:
```python
import math

import jax
import jax.numpy as jnp
import numpy as np
from jax import lax
from jax.experimental import pallas as pl
from jax.experimental.pallas import tpu as pltpu
from jax.sharding import PartitionSpec as P


def paley_matrix():
    elements = [(first_part, second_part) for first_part in range(5) for second_part in range(5)]
    squares = set()
    for left_elem in elements:
        if left_elem != (0, 0):
            squares.add(
                (
                    (left_elem[0] * left_elem[0] + 3 * left_elem[1] * left_elem[1]) % 5,
                    2 * left_elem[0] * left_elem[1] % 5,
                )
            )
    jacobs = np.zeros((25, 25))
    for row_index in range(25):
        for col_index in range(25):
            left_elem = elements[row_index]
            right_elem = elements[col_index]
            differ = ((left_elem[0] - right_elem[0]) % 5, (left_elem[1] - right_elem[1]) % 5)
            if differ == (0, 0):
                jacobs[row_index, col_index] = 0.0
            elif differ in squares:
                jacobs[row_index, col_index] = 1.0
            else:
                jacobs[row_index, col_index] = -1.0
    conference = np.zeros((26, 26))
    conference[0, 1:] = 1.0
    conference[1:, 0] = 1.0
    conference[1:, 1:] = jacobs
    result = np.kron(conference, np.array([[1.0, 1.0], [1.0, -1.0]])) + np.kron(
        np.eye(26), np.array([[1.0, -1.0], [-1.0, -1.0]])
    )
    return result


def sylvester(order):
    matrix = np.ones((1, 1))
    while matrix.shape[0] < order:
        matrix = np.kron(np.array([[1.0, 1.0], [1.0, -1.0]]), matrix)
    return matrix


def decode_weights(codes, exponents):
    magnitude = jnp.bitwise_and(codes, 7).astype(jnp.float32)
    value = jnp.where(
        magnitude < 4.0,
        magnitude * 0.5,
        jnp.where(magnitude < 6.0, magnitude - 2.0, 2.0 * magnitude - 8.0),
    )
    value = jnp.where(codes >= 8, -value, value)
    scales = jnp.where(
        exponents == 0,
        2.0 ** (-11),
        jnp.where(
            exponents == 1, 2.0 ** (-10), jnp.where(exponents == 2, 2.0 ** (-9), 2.0 ** (-8))
        ),
    ).astype(jnp.float32)
    blocks = value.reshape(codes.shape[0] // 32, 32, codes.shape[1]) * scales[:, None, :]
    return blocks.reshape(codes.shape).astype(jnp.bfloat16)


def butterfly(total, distance):
    rows, width = total.shape
    if distance % 8 == 0:
        pairs = total.reshape(rows // (2 * distance), 2, distance, width)
        low, high = pairs[:, 0], pairs[:, 1]
        return jnp.stack([low + high, low - high], axis=1).reshape(rows, width)
    tiles = total.reshape(rows // 8, 8, width)
    other = pltpu.roll(tiles, 4, 1)
    place = lax.broadcasted_iota(jnp.int32, tiles.shape, 1)
    return jnp.where(place < 4, tiles + other, other - tiles).reshape(rows, width)


def rotate_kernel(share, scaling, rows_ref, matrix_ref, out_ref):
    half = matrix_ref.shape[0]
    for start in range(0, half, 256):
        width = min(256, half - start)
        columns = matrix_ref[:, start : start + width]
        low = jnp.dot(rows_ref[:, :half], columns, preferred_element_type=jnp.float32)
        high = jnp.dot(rows_ref[:, half:], columns, preferred_element_type=jnp.float32)
        for place, total in ((0, low + high), (half, low - high)):
            distance = share
            while distance < rows_ref.shape[0]:
                total = butterfly(total, distance)
                distance *= 2
            out_ref[:, place + start : place + start + width] = (total * scaling).astype(
                jnp.bfloat16
            )


def rotate(raw, matrix):
    groups, share, width = raw.shape
    scaling = 1.0 / math.sqrt(groups * width)
    rotated = pl.pallas_call(
        lambda *refs: rotate_kernel(share, scaling, *refs),
        out_shape=jax.ShapeDtypeStruct((groups * share, width), jnp.bfloat16),
        in_specs=[pl.BlockSpec(memory_space=pltpu.VMEM)] * 2,
        out_specs=pl.BlockSpec(memory_space=pltpu.VMEM),
        compiler_params=pltpu.CompilerParams(vmem_limit_bytes=40 * 1024 * 1024),
        cost_estimate=pl.CostEstimate(
            flops=2 * groups * share * width * (width // 2),
            bytes_accessed=width * width // 2 + 4 * groups * share * width,
            transcendentals=0,
        ),
    )(raw.reshape(groups * share, width), matrix)
    return rotated.reshape(groups, share, width)


CHUNKS = 1


def shards(hidden, sign_bits, weight_codes, weight_exps):
    tokens, width = hidden.shape
    groups = lax.axis_size("tp")
    n_ctx = lax.axis_size("ctx")
    owners_here = groups // n_ctx
    piece = tokens // owners_here // CHUNKS
    matrix = jnp.asarray(np.kron(sylvester(width // 104), paley_matrix()), jnp.bfloat16)
    signed = hidden * (1 - 2 * sign_bits).astype(jnp.bfloat16)[None, :]
    cut = signed.reshape(owners_here, CHUNKS, piece, width)
    weight_down = decode_weights(weight_codes, weight_exps)
    outs = []
    for chunk in range(CHUNKS):
        raw = cut[:, chunk].reshape(groups, owners_here * piece // groups, width)
        raw = lax.all_to_all(raw, "tp", 0, 0, tiled=True)
        rotated = rotate(raw, matrix)
        rotated = lax.all_to_all(rotated, "tp", 0, 0, tiled=True)
        rotated = rotated.reshape(owners_here * piece, width)
        gathered = lax.all_gather(rotated, "ctx", axis=0, tiled=True)
        partial = jnp.dot(gathered, weight_down, preferred_element_type=jnp.float32)
        outs.append(lax.psum_scatter(partial, "tp", scatter_dimension=0, tiled=True))
    return jnp.concatenate(outs, axis=0)


def solution(mesh):
    return jax.shard_map(
        shards,
        mesh=mesh,
        in_specs=(P("ctx", "tp"), P("tp"), P("tp", "ctx"), P("tp", "ctx")),
        out_specs=P("tp", "ctx"),
        check_vma=False,
    )
```

time: 547 us -> 326 us (0.60)
  waiting for transfers between devices: 449 us -> 212 us
  blocking collectives: 0 us -> 57.4 us
  other arithmetic: 29.1 us -> 13.4 us
  local copies, waits for them, and re-layouts: 14.5 us -> 2.57 us
  matrix products: 29.8 us -> 20.1 us
  starting transfers between devices: 7.94 us -> 0.04 us
    ppermute x4 -> x0, waiting for transfers between devices: 225 us -> none  [swapped(): return lax.ppermute(block, axis, route)]
    all_to_all x0 -> x2, blocking collectives: none -> 57.4 us  [the longest x1 30.6 us: shards(): raw = lax.all_to_all(raw, 'tp', 0, 0, tiled=True)]
    all_gather x1, waiting for transfers between devices: 154 us -> 142 us  [shards(): gathered = lax.all_gather(rotated, 'ctx', axis=0, tiled=True)]
    select_n x3 -> x0, other arithmetic: 11 us -> none  [rotate(): spread = jnp.where(on_high, partner - spread, spread + partner)]
    dot_general x3 -> x1, matrix products: 29.8 us -> 20.1 us  [shards(): partial = jnp.dot(gathered, weight_down, preferred_element_type=jnp.float32)]
    ppermute x4 -> x0, starting transfers between devices: 7.89 us -> none  [swapped(): return lax.ppermute(block, axis, route)]
    reshape x2 -> x0, local copies, waits for them, and re-layouts: 7.54 us -> none  [the longest x1 4.68 us: rotate(): folded = signed.reshape(count_rows, local_order, 52)]
  transfers between devices with their start and end apart: 6 -> 2, of which waited for: 6 -> 2; matrix products, arithmetic and copies ran while one was open for 2% -> 3% of each run, Pallas kernels for 0% -> 0%
where the time goes in v1:
time: 326 us; the launch traced here: 322 us
  waiting for transfers between devices  212 us (65%)
  blocking collectives  57.4 us (18%)
  matrix products  20.1 us (6%)
  other arithmetic  13.4 us (4%)
  between operations  13.4 us (4%)
  Pallas kernels  3.59 us (1%)
    all_gather x1, waiting for transfers between devices, shards(): gathered = lax.all_gather(rotated, 'ctx', axis=0, tiled=True)  142 us
    reduce_scatter x1, waiting for transfers between devices, shards(): lax.psum_scatter(partial, 'tp', scatter_dimension=0, tiled=True)  69.7 us
    all_to_all x1, blocking collectives, shards(): raw = lax.all_to_all(raw, 'tp', 0, 0, tiled=True)  30.6 us
    all_to_all x1, blocking collectives, shards(): rotated = lax.all_to_all(rotated, 'tp', 0, 0, tiled=True)  26.9 us
    dot_general x1, matrix products, shards(): partial = jnp.dot(gathered, weight_down, preferred_element_type=jnp.float32)  20.1 us
    convert_element_type x1, other arithmetic, decode_weights(): return blocks.reshape(codes.shape).astype(jnp.bfloat16)  11 us
  transfers between devices with their start and end apart: 2, of which 2 were waited for; matrix products, arithmetic and copies ran while one was open for 3% of the time, Pallas kernels for 0%

profile of v1, /device:TPU:1, one launch (start us, length us, event | category | flops | bytes accessed | tf_op | source)
XLA Modules:
  0.0 322.3 jit_solution(5567587640619100303)
XLA Ops:
  6.5 0.0 copy-start.1
  6.5 0.0 all-gather.2.cloned.1.call-start
  6.5 0.8 subtract_convert_fusion
  7.3 1.6 broadcast_multiply_fusion
  8.9 30.6 %all_to_all.10 = bf16[16,16,3328]{2,1,0:T(8,128)(2,1)S(1)} all-to-all(bf16[16,16,3328]{2,1,0:T(8,128)(2,1)S(1)} %bitcast.11), channel_id=1, replica_groups=mesh['ctx'=8,'tp'=16] {'tp'}, dimensions={0} | all-to-all | bytes 3407872 | tf_op jit(solution)/shard_map/all_to_all | solution.py:134
  39.4 0.0 copy-start
  39.4 2.6 copy-done
  42.0 3.6 %shard_map.55 = bf16[256,3328]{1,0:T(8,128)(2,1)S(1)} custom-call(bf16[256,3328]{1,0:T(8,128)(2,1)S(1)} %bitcast.8, bf16[1664,1664]{1,0:T(8,128)(2,1)S(1)} %copy-done), custom_call_target="tpu_custom_call" | custom-call | flops 2835349504 | bytes 8945664 | tf_op jit(solution)/shard_map/pallas_call | solution.py:103
  45.6 26.9 %all_to_all.11 = bf16[16,16,3328]{2,1,0:T(8,128)(2,1)} all-to-all(bf16[16,16,3328]{2,1,0:T(8,128)(2,1)S(1)} %bitcast.9), channel_id=1, replica_groups=mesh['ctx'=8,'tp'=16] {'tp'}, dimensions={0} | all-to-all | bytes 3407872 | tf_op jit(solution)/shard_map/all_to_all | solution.py:136
  72.5 0.0 all-gather.2.cloned.1.call-update
  72.5 0.0 reduce-scatter.2.cloned.1.call-start
  72.6 0.0 copy-done.1
  72.6 0.1 select_select_fusion
  72.7 11.0 %fusion.1 = bf16[3328,1024]{1,0:T(8,128)(2,1)} fusion(s32[3328,1024]{1,0:T(8,128)} %param.7, f32[104,1024]{1,0:T(8,128)S(1)} %select_select_fusion), kind=kLoop, calls=%fused_computation.2 | loop fusion | flops 51118080 | bytes 20873216 | tf_op jit(solution)/shard_map/convert_element_type | solution.py:68
  83.6 142.0 %all-gather.2.cloned.1.call-done = bf16[2048,3328]{1,0:T(8,128)(2,1)} async-done(((bf16[256,3328]{1,0:T(8,128)(2,1)}), bf16[2048,3328]{1,0:T(8,128)(2,1)}) %all-gather.2.cloned.1.call-update) | async-done | bytes 13631504 | tf_op jit(solution)/shard_map/all_gather | solution.py:138
  225.6 20.1 %fusion.2 = f32[2048,1024]{1,0:T(8,128)} fusion(bf16[2048,3328]{1,0:T(8,128)(2,1)} %all-gather.2.cloned.1.call-done, bf16[3328,1024]{1,0:T(8,128)(2,1)} %fusion.1), kind=kOutput, calls=%fused_computation.8 | convolution fusion | flops 13958643712 | bytes 28835840 | tf_op jit(solution)/shard_map/dot_general | solution.py:139
  245.7 0.0 reduce-scatter.2.cloned.1.call-update
  245.7 69.7 %reduce-scatter.2.cloned.1.call-done = f32[128,1024]{1,0:T(8,128)} async-done(((f32[2048,1024]{1,0:T(8,128)}), f32[128,1024]{1,0:T(8,128)}) %reduce-scatter.2.cloned.1.call-update) | async-done | bytes 524304 | tf_op jit(solution)/shard_map/reduce_scatter | solution.py:140
Async XLA Ops:
  6.5 66.1 %copy-start.1 = (s32[104,1024]{1,0:T(8,128)S(1)}, s32[104,1024]{1,0:T(8,128)}, u32[]{:S(2)}) copy-start(s32[104,1024]{1,0:T(8,128)} %param.8) | copy-start | bytes 1277956
  6.5 219.1 %all-gather.2.cloned.1.call-start = ((), (), s32[]{:S(2)}) async-start(), calls=%async_computation.3 | async-start | bytes 15335424 | tf_op jit(solution)/shard_map/all_gather | solution.py:138
  39.4 2.6 copy-start
  72.5 242.9 %reduce-scatter.2.cloned.1.call-start = ((), (), s32[]{:S(2)}) async-start(), calls=%async_computation.4 | async-start | bytes 8912896 | tf_op jit(solution)/shard_map/reduce_scatter | solution.py:140
Sparse Core Ops, SparseCore 0:
  72.7 152.9 all-gather.1
  245.8 69.5 reduce-scatter.1

commit v2 on v1

v2 whole, which is shorter than its diff:
```python
import math

import jax
import jax.numpy as jnp
import numpy as np
from jax import lax
from jax.experimental import pallas as pl
from jax.experimental.pallas import tpu as pltpu
from jax.sharding import PartitionSpec as P


def paley_matrix():
    elements = [(first_part, second_part) for first_part in range(5) for second_part in range(5)]
    squares = set()
    for left_elem in elements:
        if left_elem != (0, 0):
            squares.add(
                (
                    (left_elem[0] * left_elem[0] + 3 * left_elem[1] * left_elem[1]) % 5,
                    2 * left_elem[0] * left_elem[1] % 5,
                )
            )
    jacobs = np.zeros((25, 25))
    for row_index in range(25):
        for col_index in range(25):
            left_elem = elements[row_index]
            right_elem = elements[col_index]
            differ = ((left_elem[0] - right_elem[0]) % 5, (left_elem[1] - right_elem[1]) % 5)
            if differ == (0, 0):
                jacobs[row_index, col_index] = 0.0
            elif differ in squares:
                jacobs[row_index, col_index] = 1.0
            else:
                jacobs[row_index, col_index] = -1.0
    conference = np.zeros((26, 26))
    conference[0, 1:] = 1.0
    conference[1:, 0] = 1.0
    conference[1:, 1:] = jacobs
    result = np.kron(conference, np.array([[1.0, 1.0], [1.0, -1.0]])) + np.kron(
        np.eye(26), np.array([[1.0, -1.0], [-1.0, -1.0]])
    )
    return result


def sylvester(order):
    matrix = np.ones((1, 1))
    while matrix.shape[0] < order:
        matrix = np.kron(np.array([[1.0, 1.0], [1.0, -1.0]]), matrix)
    return matrix


def decode_kernel(codes_ref, exps_ref, out_ref):
    for block in range(exps_ref.shape[0]):
        codes = codes_ref[block * 32 : block * 32 + 32, :]
        scale = jnp.left_shift(1, exps_ref[block : block + 1, :]).astype(jnp.float32) * 2.0 ** (-11)
        scale = jnp.where(codes >= 8, -scale, scale)
        magnitude = jnp.bitwise_and(codes, 7).astype(jnp.float32)
        value = jnp.where(
            magnitude < 4.0,
            magnitude * 0.5,
            jnp.where(magnitude < 6.0, magnitude - 2.0, 2.0 * magnitude - 8.0),
        )
        out_ref[block * 32 : block * 32 + 32, :] = (value * scale).astype(jnp.bfloat16)


def decode_weights(codes, exponents):
    rows, columns = codes.shape
    step = 256
    return pl.pallas_call(
        decode_kernel,
        grid=(rows // step,),
        out_shape=jax.ShapeDtypeStruct(codes.shape, jnp.bfloat16),
        in_specs=[
            pl.BlockSpec((step, columns), lambda i: (i, 0)),
            pl.BlockSpec((step // 32, columns), lambda i: (i, 0)),
        ],
        out_specs=pl.BlockSpec((step, columns), lambda i: (i, 0)),
        compiler_params=pltpu.CompilerParams(vmem_limit_bytes=56 * 1024 * 1024),
        cost_estimate=pl.CostEstimate(
            flops=10 * rows * columns, bytes_accessed=6 * rows * columns, transcendentals=0
        ),
    )(codes, exponents)


def butterfly(parts):
    distance = 1
    while distance < len(parts):
        parts = [
            parts[index] + parts[index + distance]
            if index // distance % 2 == 0
            else parts[index - distance] - parts[index]
            for index in range(len(parts))
        ]
        distance *= 2
    return parts


def rotate_kernel(share, scaling, rows_ref, matrix_ref, out_ref, total_ref, columns_ref, arrived):
    half = matrix_ref.shape[0]
    starts = list(range(0, half, 256))
    copies = []
    for index, start in enumerate(starts):
        window = pl.ds(start, min(256, half - start))
        copies.append(
            pltpu.make_async_copy(
                matrix_ref.at[:, window], columns_ref.at[:, window], arrived.at[index]
            )
        )
    for copy in copies:
        copy.start()
    stacked = jnp.concatenate([rows_ref[:, :half], rows_ref[:, half:]], axis=0)
    for index, start in enumerate(starts):
        width = min(256, half - start)
        copies[index].wait()
        columns = columns_ref[:, start : start + width]
        total_ref[:, :width] = jnp.dot(stacked, columns, preferred_element_type=jnp.float32)
        count = rows_ref.shape[0]
        for lane in range(0, width, 128):
            low, high = (
                [
                    total_ref[base + at : base + at + share, lane : lane + 128]
                    for at in range(0, count, share)
                ]
                for base in (0, count)
            )
            window = slice(start + lane, start + lane + 128)
            other = slice(half + start + lane, half + start + lane + 128)
            for at, (one, two) in enumerate(zip(butterfly(low), butterfly(high))):
                out_ref[at, :, window] = ((one + two) * scaling).astype(jnp.bfloat16)
                out_ref[at, :, other] = ((one - two) * scaling).astype(jnp.bfloat16)


def rotate(raw, matrix):
    groups, share, width = raw.shape
    scaling = 1.0 / math.sqrt(groups * width)
    return pl.pallas_call(
        lambda *refs: rotate_kernel(share, scaling, *refs),
        out_shape=jax.ShapeDtypeStruct(raw.shape, jnp.bfloat16),
        in_specs=[
            pl.BlockSpec(memory_space=pltpu.VMEM),
            pl.BlockSpec(memory_space=pl.ANY),
        ],
        out_specs=pl.BlockSpec(memory_space=pltpu.VMEM),
        scratch_shapes=[
            pltpu.VMEM((2 * groups * share, 256), jnp.float32),
            pltpu.VMEM(matrix.shape, jnp.bfloat16),
            pltpu.SemaphoreType.DMA((-(-matrix.shape[0] // 256),)),
        ],
        compiler_params=pltpu.CompilerParams(vmem_limit_bytes=56 * 1024 * 1024),
        cost_estimate=pl.CostEstimate(
            flops=2 * groups * share * width * (width // 2),
            bytes_accessed=width * width // 2 + 4 * groups * share * width,
            transcendentals=0,
        ),
    )(raw.reshape(groups * share, width), matrix)


def block_of(place_ref, shift):
    return lax.rem(place_ref[0] + shift[0], 4) * 2 + lax.rem(place_ref[1] + shift[1], 2)


def product_kernel(spec, shifts, place_ref, weight_ref, *refs):
    pieces = refs[:-3]
    out_ref, rows_ref, arrived = refs[-3:]
    blocks, n_rows, width = rows_ref.shape

    @pl.when(pl.program_id(0) == 0)
    def _():
        copies = []
        for index, (source, begin, count, block, start) in enumerate(spec):
            window = rows_ref.at[block, pl.ds(start, count)]
            block_rows = pieces[source].at[pl.ds(begin, count)]
            copies.append(pltpu.make_async_copy(block_rows, window, arrived.at[index]))
        for copy in copies:
            copy.start()
        for copy in copies:
            copy.wait()

    total = (
        jnp.dot(
            rows_ref[...].reshape(blocks * n_rows, width),
            weight_ref[...],
            preferred_element_type=jnp.float32,
        )
        .reshape(blocks, n_rows, weight_ref.shape[1])
        .astype(jnp.bfloat16)
    )
    for block, shift in enumerate(shifts):
        out_ref[block_of(place_ref, shift)] = total[block]


def product(place, weight, spec, pieces):
    width, columns = weight.shape
    tile = 256
    blocks = 7
    rows = sum(piece.shape[0] for piece in pieces) // blocks
    shifts = [(0, 0), (3, 0), (1, 0), (2, 0), (0, 1), (3, 1), (1, 1)]
    return pl.pallas_call(
        lambda *refs: product_kernel(spec, shifts, *refs),
        grid=(columns // tile,),
        out_shape=jax.ShapeDtypeStruct((blocks + 1, rows, columns), jnp.bfloat16),
        in_specs=[
            pl.BlockSpec(memory_space=pltpu.SMEM),
            pl.BlockSpec((width, tile), lambda i: (0, i)),
        ]
        + [pl.BlockSpec(memory_space=pl.ANY)] * len(pieces),
        out_specs=pl.BlockSpec((blocks + 1, rows, tile), lambda i: (0, 0, i)),
        scratch_shapes=[
            pltpu.VMEM((blocks, rows, width), jnp.bfloat16),
            pltpu.SemaphoreType.DMA((len(spec),)),
        ],
        compiler_params=pltpu.CompilerParams(vmem_limit_bytes=56 * 1024 * 1024),
        cost_estimate=pl.CostEstimate(
            flops=50 * blocks * rows * width * columns,
            bytes_accessed=2 * (width * columns + blocks * rows * (width + columns)),
            transcendentals=0,
        ),
    )(place, weight, *pieces)


def last_kernel(place_ref, weight_ref, before_ref, low_ref, high_ref, out_ref, rows_ref, total_ref, arrived):
    step = pl.program_id(0)
    half = low_ref.shape[0]
    tile = weight_ref.shape[1]

    @pl.when(step == 0)
    def _():
        rows_ref[:half] = low_ref[...]
        rows_ref[half:] = high_ref[...]

    total_ref[step] = jnp.dot(
        rows_ref[...], weight_ref[...], preferred_element_type=jnp.float32
    ).astype(jnp.bfloat16)

    @pl.when(step == total_ref.shape[0] - 1)
    def _():
        copies = []
        for index in range(total_ref.shape[0]):
            window = out_ref.at[block_of(place_ref, (2, 1)), :, pl.ds(index * tile, tile)]
            copies.append(pltpu.make_async_copy(total_ref.at[index], window, arrived.at[index]))
        for copy in copies:
            copy.start()
        for copy in copies:
            copy.wait()


def product_last(place, weight, before, low, high):
    width, columns = weight.shape
    tile = 256
    rows = 2 * low.shape[0]
    return pl.pallas_call(
        last_kernel,
        grid=(columns // tile,),
        out_shape=jax.ShapeDtypeStruct(before.shape, jnp.bfloat16),
        in_specs=[
            pl.BlockSpec(memory_space=pltpu.SMEM),
            pl.BlockSpec((width, tile), lambda i: (0, i)),
            pl.BlockSpec(memory_space=pl.ANY),
            pl.BlockSpec(low.shape, lambda i: (0, 0)),
            pl.BlockSpec(high.shape, lambda i: (0, 0)),
        ],
        out_specs=pl.BlockSpec(memory_space=pl.ANY),
        scratch_shapes=[
            pltpu.VMEM((rows, width), jnp.bfloat16),
            pltpu.VMEM((columns // tile, rows, tile), jnp.bfloat16),
            pltpu.SemaphoreType.DMA((columns // tile,)),
        ],
        input_output_aliases={2: 0},
        compiler_params=pltpu.CompilerParams(vmem_limit_bytes=56 * 1024 * 1024),
        cost_estimate=pl.CostEstimate(
            flops=2 * rows * width * columns,
            bytes_accessed=2 * (width * columns + rows * (width + columns)),
            transcendentals=0,
        ),
    )(place, weight, before, low, high)


def ring(step):
    def move(block):
        count = lax.axis_size("ctx")
        return lax.ppermute(block, "ctx", [(i, (i + 2 * step) % count) for i in range(count)])

    return move


def across(block):
    return lax.ppermute(block, "ctx", [(i, i ^ 1) for i in range(lax.axis_size("ctx"))])


def exchange(block):
    return lax.all_to_all(block, "tp", 0, 0, tiled=True)


def sync(*values):
    return lax.optimization_barrier(values)


def keep(*values):
    return values

def shards(hidden, sign_bits, weight_codes, weight_exps):
    tokens, width = hidden.shape
    columns = weight_codes.shape[1]
    groups = lax.axis_size("tp")
    share = tokens // groups // 2
    matrix = jnp.asarray(np.kron(sylvester(width // 104), paley_matrix()), jnp.bfloat16)
    flips = (1 - 2 * sign_bits).astype(jnp.bfloat16)
    ctx = lax.axis_index("ctx")
    place = jnp.stack([ctx // 2, ctx % 2]).astype(jnp.int32)
    up, down = ring(1), ring(-1)
    rows = tokens // 2
    half, quarter = rows // 2, rows // 4
    got = exchange((hidden * flips).reshape(groups, 2 * share, width))
    weight = decode_weights(weight_codes, weight_exps)
    got, weight = sync(got, weight)
    own0 = exchange(rotate(got[:, :share], matrix)).reshape(rows, width)
    rotated1 = rotate(got[:, share:], matrix)
    own0, rotated1, weight = keep(own0, rotated1, weight)

    below0, above0, other0 = up(own0), down(own0), across(own0)
    own1 = exchange(rotated1).reshape(rows, width)
    below0, above0, other0, own1, weight = keep(below0, above0, other0, own1, weight)

    other_below0, other_above0 = up(other0[:half]), down(other0[:half])
    far0 = [up(below0[:half]), down(above0[half:])]
    late0 = across(jnp.concatenate([below0[half:], above0[half:]]))
    other_below0, other_above0, late0, own1, *far0 = keep(
        other_below0, other_above0, late0, own1, *far0
    )

    spec = [
        (0, 0, rows, 0, 0),
        (1, 0, rows, 1, 0),
        (2, 0, rows, 2, 0),
        (3, 0, half, 3, 0),
        (4, 0, half, 3, half),
        (5, 0, rows, 4, 0),
        (6, 0, half, 5, 0),
        (7, 0, half, 6, 0),
        (8, 0, half, 5, half),
        (8, half, half, 6, half),
    ]
    last0 = up(other_below0)
    late_far0 = across(far0[1])
    below1, above1, other1 = up(own1), down(own1), across(own1)
    pieces0 = [own0, below0, above0, *far0, other0, other_below0, other_above0, late0]
    part0 = product(place, weight, spec, pieces0)
    below1, above1, other1, late_far0, part0, last0 = keep(
        below1, above1, other1, late_far0, part0, last0
    )

    part0 = product_last(place, weight, part0, last0, late_far0)
    sent0 = exchange(part0.reshape(groups, half, columns))
    other_below1, other_above1 = up(other1), down(other1)
    far1 = [up(below1[:half]), down(above1[half:])]
    other_below1, other_above1, *far1 = keep(other_below1, other_above1, *far1)

    last1 = [up(other_below1[:half]), down(other_above1[half:])]
    spec1 = [(0, 0, rows, 0, 0), (1, 0, rows, 1, 0), (2, 0, rows, 2, 0), (3, 0, half, 3, 0)]
    spec1 += [(4, 0, half, 3, half), (5, 0, rows, 4, 0), (6, 0, rows, 5, 0), (7, 0, rows, 6, 0)]
    pieces1 = [own1, below1, above1, *far1, other1, other_below1, other_above1]
    part1 = product(place, weight, spec1, pieces1)
    part1, *last1 = keep(part1, *last1)
    part1 = product_last(place, weight, part1, *last1)
    sent1 = exchange(part1.reshape(groups, half, columns))
    outs = [
        jnp.sum(sent.astype(jnp.float32), axis=0).reshape(groups // 2, share, columns)
        for sent in (sent0, sent1)
    ]
    return jnp.concatenate(outs, axis=1).reshape(rows, columns)


def solution(mesh):
    return jax.shard_map(
        shards,
        mesh=mesh,
        in_specs=(P("ctx", "tp"), P("tp"), P("tp", "ctx"), P("tp", "ctx")),
        out_specs=P("tp", "ctx"),
        check_vma=False,
    )
```

time: 326 us -> 237 us (0.73)
  waiting for transfers between devices: 212 us -> 82.4 us
  Pallas kernels: 3.59 us -> 64.8 us
  starting transfers between devices: 0.04 us -> 50.9 us
  blocking collectives: 57.4 us -> 18.4 us
  matrix products: 20.1 us -> 0 us
  between operations: 13.4 us -> 0.19 us
  local copies, waits for them, and re-layouts: 2.57 us -> 11.5 us
  other arithmetic: 13.4 us -> 7.46 us
    all_gather x1 -> x0, waiting for transfers between devices: 142 us -> none  [shards(): gathered = lax.all_gather(rotated, 'ctx', axis=0, tiled=True)]
    reduce_scatter x1 -> x0, waiting for transfers between devices: 69.7 us -> none  [shards(): lax.psum_scatter(partial, 'tp', scatter_dimension=0, tiled=True)]
    all_to_all x0 -> x4, waiting for transfers between devices: none -> 53.5 us  [exchange(): return lax.all_to_all(block, 'tp', 0, 0, tiled=True)]
    pallas_call x0 -> x5, Pallas kernels: none -> 49.4 us  [the longest x2 24.3 us: product(): pl.pallas_call(lambda *refs: product_kernel(spec, shifts, *refs), grid=(c...]
    all_to_all x2 -> x1, blocking collectives: 57.4 us -> 18.4 us  [exchange(): return lax.all_to_all(block, 'tp', 0, 0, tiled=True)]
    ppermute x0 -> x19, waiting for transfers between devices: none -> 28.9 us  [the longest x15 17.5 us: move(): lax.ppermute(block, 'ctx', [(i, (i + 2 * step) % count) for i in range(co...]
    all_to_all x0 -> x4, starting transfers between devices: none -> 28.7 us  [exchange(): return lax.all_to_all(block, 'tp', 0, 0, tiled=True)]
    ppermute x0 -> x19, starting transfers between devices: none -> 22.2 us  [the longest x15 15.4 us: move(): lax.ppermute(block, 'ctx', [(i, (i + 2 * step) % count) for i in range(co...]
  transfers between devices with their start and end apart: 2 -> 23, of which waited for: 2 -> 8; matrix products, arithmetic and copies ran while one was open for 3% -> 5% of each run, Pallas kernels for 0% -> 24%
where the time goes in v2:
time: 237 us; the launch traced here: 236 us
  waiting for transfers between devices  82.4 us (35%)
  Pallas kernels  64.8 us (27%)
  starting transfers between devices  50.9 us (21%)
  blocking collectives  18.4 us (8%)
  local copies, waits for them, and re-layouts  11.5 us (5%)
  other arithmetic  7.46 us (3%)
    all_to_all x4, waiting for transfers between devices, exchange(): return lax.all_to_all(block, 'tp', 0, 0, tiled=True)  53.5 us
    all_to_all x4, starting transfers between devices, exchange(): return lax.all_to_all(block, 'tp', 0, 0, tiled=True)  28.7 us
    pallas_call x2, Pallas kernels, product(): pl.pallas_call(lambda *refs: product_kernel(spec, shifts, *refs), grid=(c...  24.3 us
    all_to_all x1, blocking collectives, exchange(): return lax.all_to_all(block, 'tp', 0, 0, tiled=True)  18.4 us
    ppermute x15, waiting for transfers between devices, move(): lax.ppermute(block, 'ctx', [(i, (i + 2 * step) % count) for i in range(co...  17.5 us
    ppermute x15, starting transfers between devices, move(): lax.ppermute(block, 'ctx', [(i, (i + 2 * step) % count) for i in range(co...  15.4 us
    pallas_call x2, Pallas kernels, rotate(): pl.pallas_call(lambda *refs: rotate_kernel(share, scaling, *refs), out_sh...  15.3 us
    pallas_call x1, Pallas kernels, decode_weights(): pl.pallas_call(decode_kernel, grid=(rows // step,), out_shape=jax.ShapeDt...  14.3 us
  transfers between devices with their start and end apart: 23, of which 8 were waited for; matrix products, arithmetic and copies ran while one was open for 5% of the time, Pallas kernels for 24%

profile of v2, /device:TPU:1, one launch (start us, length us, event | category | flops | bytes accessed | tf_op | source)
XLA Modules:
  0.0 235.7 jit_solution(16270430581776914359)
XLA Ops:
  0.7 2.9 %broadcast_multiply_fusion = bf16[256,3328]{1,0:T(8,128)(2,1)} fusion(bf16[256,3328]{1,0:T(8,128)(2,1)} %param.5, bf16[3328]{0:T(1024)(128)(2,1)S(1)} %subtract_convert_fusion), kind=kLoop, calls=%fused_computation.5 | loop fusion | flops 851968 | bytes 3414528 | tf_op jit(solution)/shard_map/mul | solution.py:313
  3.6 7.8 %all-to-all-start = ((bf16[16,16,3328]{2,1,0:T(8,128)(2,1)}), bf16[16,16,3328]{2,1,0:T(8,128)(2,1)S(1)}, u32[]{:S(2)}, u32[]{:S(2)}) async-start(bf16[16,16,3328]{2,1,0:T(8,128)(2,1)} %bitcast.2), calls=%async_computation | async-start | bytes 3407872 | tf_op jit(solution)/shard_map/all_to_all | solution.py:291
  11.3 14.3 %shard_map.55.refs_1_.weight_ref = bf16[3328,1024]{1,0:T(8,128)(2,1)} custom-call(s32[3328,1024]{1,0:T(8,128)} %codes_ref.1, s32[104,1024]{1,0:T(8,128)} %exps_ref.1), custom_call_target="tpu_custom_call" | custom-call | flops 34078720 | bytes 20447232 | tf_op jit(solution)/shard_map/pallas_call | solution.py:69
  25.6 9.0 %all-to-all-done = bf16[16,16,3328]{2,1,0:T(8,128)(2,1)S(1)} async-done(((bf16[16,16,3328]{2,1,0:T(8,128)(2,1)}), bf16[16,16,3328]{2,1,0:T(8,128)(2,1)S(1)}, u32[]{:S(2)}, u32[]{:S(2)}) %all-to-all-start) | async-done | bytes 1703968 | tf_op jit(solution)/shard_map/all_to_all | solution.py:291
  36.0 7.6 %shard_map.56 = bf16[16,8,3328]{2,1,0:T(8,128)(2,1)} custom-call(bf16[128,3328]{1,0:T(8,128)(2,1)} %get-tuple-element.9.refs_0_, bf16[1664,1664]{1,0:T(8,128)(2,1)} %constant.36.clone.refs_1_), custom_call_target="tpu_custom_call" | custom-call | flops 1417674752 | bytes 7241728 | tf_op jit(solution)/shard_map/pallas_call | solution.py:136
  43.7 18.4 %all_to_all.25 = bf16[16,8,3328]{2,1,0:T(8,128)(2,1)S(1)} all-to-all(bf16[16,8,3328]{2,1,0:T(8,128)(2,1)} %shard_map.56), channel_id=1, replica_groups=mesh['ctx'=8,'tp'=16] {'tp'}, dimensions={0} | all-to-all | bytes 1703936 | tf_op jit(solution)/shard_map/all_to_all | solution.py:291
  63.4 2.5 %collective-permute-start.4 = (bf16[128,3328]{1,0:T(8,128)(2,1)S(1)}, bf16[128,3328]{1,0:T(8,128)(2,1)}, u32[]{:S(2)}, u32[]{:S(2)}) collective-permute-start(bf16[128,3328]{1,0:T(8,128)(2,1)S(1)} %bitcast.23), channel_id=1, source_target_pairs={{0,16},{16,0},{32,48},{48,32},{64,80},{80,64},{96,112},{112,96},{1... | collective-permute-start | bytes 2555912 | tf_op jit(solution)/shard_map/ppermute | solution.py:287
  65.9 7.7 %shard_map.59 = bf16[16,8,3328]{2,1,0:T(8,128)(2,1)} custom-call(bf16[128,3328]{1,0:T(8,128)(2,1)} %get-tuple-element.10.refs_0_, bf16[1664,1664]{1,0:T(8,128)(2,1)} %constant.36.clone.refs_1_), custom_call_target="tpu_custom_call" | custom-call | flops 1417674752 | bytes 7241728 | tf_op jit(solution)/shard_map/pallas_call | solution.py:136
  73.6 5.1 %all-to-all-start.3 = ((bf16[16,8,3328]{2,1,0:T(8,128)(2,1)}), bf16[16,8,3328]{2,1,0:T(8,128)(2,1)S(1)}, u32[]{:S(2)}, u32[]{:S(2)}) async-start(bf16[16,8,3328]{2,1,0:T(8,128)(2,1)} %shard_map.59), calls=%async_computation.3 | async-start | bytes 1703936 | tf_op jit(solution)/shard_map/all_to_all | solution.py:291
  78.7 1.4 collective-permute-start.1
  80.2 14.2 %all-to-all-done.3 = bf16[16,8,3328]{2,1,0:T(8,128)(2,1)S(1)} async-done(((bf16[16,8,3328]{2,1,0:T(8,128)(2,1)}), bf16[16,8,3328]{2,1,0:T(8,128)(2,1)S(1)}, u32[]{:S(2)}, u32[]{:S(2)}) %all-to-all-start.3) | async-done | bytes 852000 | tf_op jit(solution)/shard_map/all_to_all | solution.py:291
  94.3 1.7 collective-permute-start.14
  103.3 11.4 %collective-permute-done.14.refs_7_ = bf16[128,3328]{1,0:T(8,128)(2,1)S(1)} collective-permute-done((bf16[128,3328]{1,0:T(8,128)(2,1)S(1)}, bf16[128,3328]{1,0:T(8,128)(2,1)S(1)}, u32[]{:S(2)}, u32[]{:S(2)}) %collective-permute-start.14) | collective-permute-done | bytes 852000 | tf_op jit(solution)/shard_map/ppermute | solution.py:287
  114.6 1.6 collective-permute-start.3
  116.2 2.7 %collective-permute-start.6 = (bf16[64,3328]{1,0:T(8,128)(2,1)S(1)}, bf16[64,3328]{1,0:T(8,128)(2,1)S(1)}, u32[]{:S(2)}, u32[]{:S(2)}) collective-permute-start(bf16[64,3328]{1,0:T(8,128)(2,1)S(1)} %slice.44), channel_id=1, source_target_pairs={{0,96},{16,112},{32,0},{48,16},{64,32},{80,48},{96,64},{112,80},{1... | collective-permute-start | bytes 1277960 | tf_op jit(solution)/shard_map/ppermute | solution.py:281
  118.9 6.1 %collective-permute-done.5.refs_8_ = bf16[64,3328]{1,0:T(8,128)(2,1)} collective-permute-done((bf16[64,3328]{1,0:T(8,128)(2,1)S(1)}, bf16[64,3328]{1,0:T(8,128)(2,1)}, u32[]{:S(2)}, u32[]{:S(2)}) %collective-permute-start.5) | collective-permute-done | bytes 426016 | tf_op jit(solution)/shard_map/ppermute | solution.py:281
  125.7 1.8 slice.46
  127.5 1.8 slice.47
  130.3 3.8 %collective-permute-done.2.refs_5_ = bf16[64,3328]{1,0:T(8,128)(2,1)S(1)} collective-permute-done((bf16[64,3328]{1,0:T(8,128)(2,1)}, bf16[64,3328]{1,0:T(8,128)(2,1)S(1)}, u32[]{:S(2)}, u32[]{:S(2)}) %collective-permute-start.2) | collective-permute-done | bytes 426016 | tf_op jit(solution)/shard_map/ppermute | solution.py:281
  135.6 7.5 %collective-permute-done.8.low_ref = bf16[64,3328]{1,0:T(8,128)(2,1)S(1)} collective-permute-done((bf16[64,3328]{1,0:T(8,128)(2,1)}, bf16[64,3328]{1,0:T(8,128)(2,1)S(1)}, u32[]{:S(2)}, u32[]{:S(2)}) %collective-permute-start.8) | collective-permute-done | bytes 426016 | tf_op jit(solution)/shard_map/ppermute | solution.py:281
  144.8 12.1 %shard_map.57.before_ref = bf16[8,128,1024]{2,1,0:T(8,128)(2,1)} custom-call(s32[2]{0:T(128)} %pad_add_fusion.refs_0_.place_ref, bf16[3328,1024]{1,0:T(8,128)(2,1)} %shard_map.55.refs_1_.weight_ref, bf16[128,3328]{1,0:T(8,128)(2,1)} %bitcast.25, bf16[128,3328]{1,0:T(8,128)(2,1)} %copy-done.2, bf16[128,3328]{1,0:T(8,128)(2,1)} %collective-permute-done.1.refs_4_, ...), custom_call_target="tpu_custom_call" | custom-call | flops 152672665600 | bytes 14614528 | tf_op jit(solution)/shard_map/pallas_call | solution.py:198
  157.0 5.4 %shard_map.58 = bf16[8,128,1024]{2,1,0:T(8,128)(2,1)} custom-call(s32[2]{0:T(128)} %pad_add_fusion.refs_0_.place_ref, bf16[3328,1024]{1,0:T(8,128)(2,1)} %shard_map.55.refs_1_.weight_ref, bf16[8,128,1024]{2,1,0:T(8,128)(2,1)} %shard_map.57.before_ref, bf16[64,3328]{1,0:T(8,128)(2,1)} %copy-done.3, ...), custom_call_target="tpu_custom_call", output_to_operand_aliasing={{}: (2, {})} | custom-call | flops 872415232 | bytes 7929856 | tf_op jit(solution)/shard_map/pallas_call | solution.py:251
  162.4 9.9 %all-to-all-start.2 = ((bf16[16,64,1024]{2,1,0:T(8,128)(2,1)}), bf16[16,64,1024]{2,1,0:T(8,128)(2,1)}, u32[]{:S(2)}, u32[]{:S(2)}) async-start(bf16[16,64,1024]{2,1,0:T(8,128)(2,1)} %bitcast.15), calls=%async_computation.2 | async-start | bytes 4194304 | tf_op jit(solution)/shard_map/all_to_all | solution.py:291
  172.3 1.8 slice.48
  175.3 1.8 slice.49
  177.1 1.4 collective-permute-start.18
  178.6 12.2 %shard_map.60.before_ref = bf16[8,128,1024]{2,1,0:T(8,128)(2,1)} custom-call(s32[2]{0:T(128)} %pad_add_fusion.refs_0_.place_ref, bf16[3328,1024]{1,0:T(8,128)(2,1)} %shard_map.55.refs_1_.weight_ref, bf16[128,3328]{1,0:T(8,128)(2,1)} %bitcast.21, bf16[128,3328]{1,0:T(8,128)(2,1)} %copy-done.4, bf16[128,3328]{1,0:T(8,128)(2,1)} %copy-done.5, ...), custom_call_target="tpu_custom_call" | custom-call | flops 152672665600 | bytes 14614528 | tf_op jit(solution)/shard_map/pallas_call | solution.py:198
  190.8 5.4 %shard_map.61 = bf16[8,128,1024]{2,1,0:T(8,128)(2,1)} custom-call(s32[2]{0:T(128)} %pad_add_fusion.refs_0_.place_ref, bf16[3328,1024]{1,0:T(8,128)(2,1)} %shard_map.55.refs_1_.weight_ref, bf16[8,128,1024]{2,1,0:T(8,128)(2,1)} %shard_map.60.before_ref, bf16[64,3328]{1,0:T(8,128)(2,1)} %collective-permute-done.17.low_ref, ...), custom_call_target="tpu_custom_call", output_to_operand_aliasing={{}: (2, {})} | custom-call | flops 872415232 | bytes 7929856 | tf_op jit(solution)/shard_map/pallas_call | solution.py:251
  196.2 4.3 %all-to-all-done.2 = bf16[16,64,1024]{2,1,0:T(8,128)(2,1)} async-done(((bf16[16,64,1024]{2,1,0:T(8,128)(2,1)}), bf16[16,64,1024]{2,1,0:T(8,128)(2,1)}, u32[]{:S(2)}, u32[]{:S(2)}) %all-to-all-start.2) | async-done | bytes 2097184 | tf_op jit(solution)/shard_map/all_to_all | solution.py:291
  200.5 6.0 %all-to-all-start.4 = ((bf16[16,64,1024]{2,1,0:T(8,128)(2,1)}), bf16[16,64,1024]{2,1,0:T(8,128)(2,1)S(1)}, u32[]{:S(2)}, u32[]{:S(2)}) async-start(bf16[16,64,1024]{2,1,0:T(8,128)(2,1)} %bitcast.14), calls=%async_computation.4 | async-start | bytes 4194304 | tf_op jit(solution)/shard_map/all_to_all | solution.py:291
  206.5 2.0 convert_reduce_fusion.1
  208.5 26.0 %all-to-all-done.4 = bf16[16,64,1024]{2,1,0:T(8,128)(2,1)S(1)} async-done(((bf16[16,64,1024]{2,1,0:T(8,128)(2,1)}), bf16[16,64,1024]{2,1,0:T(8,128)(2,1)S(1)}, u32[]{:S(2)}, u32[]{:S(2)}) %all-to-all-start.4) | async-done | bytes 2097184 | tf_op jit(solution)/shard_map/all_to_all | solution.py:291
  (55 shorter events, 17.8 us)
Async XLA Ops:
  3.6 31.1 %all-to-all-start = ((bf16[16,16,3328]{2,1,0:T(8,128)(2,1)}), bf16[16,16,3328]{2,1,0:T(8,128)(2,1)S(1)}, u32[]{:S(2)}, u32[]{:S(2)}) async-start(bf16[16,16,3328]{2,1,0:T(8,128)(2,1)} %bitcast.2), calls=%async_computation | async-start | bytes 3407872 | tf_op jit(solution)/shard_map/all_to_all | solution.py:291
  62.1 16.6 %copy-start.1 = (bf16[16,8,3328]{2,1,0:T(8,128)(2,1)}, bf16[16,8,3328]{2,1,0:T(8,128)(2,1)S(1)}, u32[]{:S(2)}) copy-start(bf16[16,8,3328]{2,1,0:T(8,128)(2,1)S(1)} %all_to_all.25) | copy-start | bytes 2555908
  62.1 37.6 %collective-permute-start = (bf16[128,3328]{1,0:T(8,128)(2,1)S(1)}, bf16[128,3328]{1,0:T(8,128)(2,1)S(1)}, u32[]{:S(2)}, u32[]{:S(2)}) collective-permute-start(bf16[128,3328]{1,0:T(8,128)(2,1)S(1)} %bitcast.22), channel_id=1, source_target_pairs={{0,32},{16,48},{32,64},{48,80},{64,96},{80,112},{96,0},{112,16},{1... | collective-permute-start | bytes 2555912 | tf_op jit(solution)/shard_map/ppermute | solution.py:281
  63.4 33.9 %collective-permute-start.4 = (bf16[128,3328]{1,0:T(8,128)(2,1)S(1)}, bf16[128,3328]{1,0:T(8,128)(2,1)}, u32[]{:S(2)}, u32[]{:S(2)}) collective-permute-start(bf16[128,3328]{1,0:T(8,128)(2,1)S(1)} %bitcast.23), channel_id=1, source_target_pairs={{0,16},{16,0},{32,48},{48,32},{64,80},{80,64},{96,112},{112,96},{1... | collective-permute-start | bytes 2555912 | tf_op jit(solution)/shard_map/ppermute | solution.py:287
  73.6 20.8 %all-to-all-start.3 = ((bf16[16,8,3328]{2,1,0:T(8,128)(2,1)}), bf16[16,8,3328]{2,1,0:T(8,128)(2,1)S(1)}, u32[]{:S(2)}, u32[]{:S(2)}) async-start(bf16[16,8,3328]{2,1,0:T(8,128)(2,1)} %shard_map.59), calls=%async_computation.3 | async-start | bytes 1703936 | tf_op jit(solution)/shard_map/all_to_all | solution.py:291
  78.7 22.1 %collective-permute-start.1 = (bf16[128,3328]{1,0:T(8,128)(2,1)S(1)}, bf16[128,3328]{1,0:T(8,128)(2,1)}, u32[]{:S(2)}, u32[]{:S(2)}) collective-permute-start(bf16[128,3328]{1,0:T(8,128)(2,1)S(1)} %bitcast.24), channel_id=1, source_target_pairs={{0,96},{16,112},{32,0},{48,16},{64,32},{80,48},{96,64},{112,80},{1... | collective-permute-start | bytes 2555912 | tf_op jit(solution)/shard_map/ppermute | solution.py:281
  94.3 7.6 %copy-start = (bf16[16,8,3328]{2,1,0:T(8,128)(2,1)}, bf16[16,8,3328]{2,1,0:T(8,128)(2,1)S(1)}, u32[]{:S(2)}) copy-start(bf16[16,8,3328]{2,1,0:T(8,128)(2,1)S(1)} %all-to-all-done.3) | copy-start | bytes 2555908
  94.3 20.3 %collective-permute-start.14 = (bf16[128,3328]{1,0:T(8,128)(2,1)S(1)}, bf16[128,3328]{1,0:T(8,128)(2,1)S(1)}, u32[]{:S(2)}, u32[]{:S(2)}) collective-permute-start(bf16[128,3328]{1,0:T(8,128)(2,1)S(1)} %bitcast.18), channel_id=1, source_target_pairs={{0,16},{16,0},{32,48},{48,32},{64,80},{80,64},{96,112},{112,96},{1... | collective-permute-start | bytes 2555912 | tf_op jit(solution)/shard_map/ppermute | solution.py:287
  96.1 20.2 %collective-permute-start.10 = (bf16[128,3328]{1,0:T(8,128)(2,1)S(1)}, bf16[128,3328]{1,0:T(8,128)(2,1)S(1)}, u32[]{:S(2)}, u32[]{:S(2)}) collective-permute-start(bf16[128,3328]{1,0:T(8,128)(2,1)S(1)} %bitcast.19), channel_id=1, source_target_pairs={{0,32},{16,48},{32,64},{48,80},{64,96},{80,112},{96,0},{112,16},{1... | collective-permute-start | bytes 2555912 | tf_op jit(solution)/shard_map/ppermute | solution.py:281
  97.4 18.9 %collective-permute-start.11 = (bf16[128,3328]{1,0:T(8,128)(2,1)S(1)}, bf16[128,3328]{1,0:T(8,128)(2,1)S(1)}, u32[]{:S(2)}, u32[]{:S(2)}) collective-permute-start(bf16[128,3328]{1,0:T(8,128)(2,1)S(1)} %bitcast.20), channel_id=1, source_target_pairs={{0,96},{16,112},{32,0},{48,16},{64,32},{80,48},{96,64},{112,80},{1... | collective-permute-start | bytes 2555912 | tf_op jit(solution)/shard_map/ppermute | solution.py:281
  99.8 2.2 copy-start.2
  99.8 25.2 %collective-permute-start.5 = (bf16[64,3328]{1,0:T(8,128)(2,1)S(1)}, bf16[64,3328]{1,0:T(8,128)(2,1)}, u32[]{:S(2)}, u32[]{:S(2)}) collective-permute-start(bf16[64,3328]{1,0:T(8,128)(2,1)S(1)} %slice.44), channel_id=1, source_target_pairs={{0,32},{16,48},{32,64},{48,80},{64,96},{80,112},{96,0},{112,16},{1... | collective-permute-start | bytes 1277960 | tf_op jit(solution)/shard_map/ppermute | solution.py:281
  101.9 41.6 %collective-permute-start.7 = (bf16[128,3328]{1,0:T(8,128)(2,1)S(1)}, bf16[128,3328]{1,0:T(8,128)(2,1)}, u32[]{:S(2)}, u32[]{:S(2)}) collective-permute-start(bf16[128,3328]{1,0:T(8,128)(2,1)S(1)} %pad_maximum_fusion), channel_id=1, source_target_pairs={{0,16},{16,0},{32,48},{48,32},{64,80},{80,64},{96,112},{112,96},{1... | collective-permute-start | bytes 2555912 | tf_op jit(solution)/shard_map/ppermute | solution.py:287
  114.6 10.5 %copy-start.6 = (bf16[128,3328]{1,0:T(8,128)(2,1)}, bf16[128,3328]{1,0:T(8,128)(2,1)S(1)}, u32[]{:S(2)}) copy-start(bf16[128,3328]{1,0:T(8,128)(2,1)S(1)} %collective-permute-done.14.refs_7_) | copy-start | bytes 2555908
  114.6 14.7 %collective-permute-start.3 = (bf16[64,3328]{1,0:T(8,128)(2,1)S(1)}, bf16[64,3328]{1,0:T(8,128)(2,1)}, u32[]{:S(2)}, u32[]{:S(2)}) collective-permute-start(bf16[64,3328]{1,0:T(8,128)(2,1)S(1)} %slice.43), channel_id=1, source_target_pairs={{0,96},{16,112},{32,0},{48,16},{64,32},{80,48},{96,64},{112,80},{1... | collective-permute-start | bytes 1277960 | tf_op jit(solution)/shard_map/ppermute | solution.py:281
  116.2 8.8 %copy-start.4 = (bf16[128,3328]{1,0:T(8,128)(2,1)}, bf16[128,3328]{1,0:T(8,128)(2,1)S(1)}, u32[]{:S(2)}) copy-start(bf16[128,3328]{1,0:T(8,128)(2,1)S(1)} %collective-permute-done.10.refs_3_) | copy-start | bytes 2555908
  116.2 17.9 %collective-permute-start.2 = (bf16[64,3328]{1,0:T(8,128)(2,1)}, bf16[64,3328]{1,0:T(8,128)(2,1)S(1)}, u32[]{:S(2)}, u32[]{:S(2)}) collective-permute-start(bf16[64,3328]{1,0:T(8,128)(2,1)} %get-tuple-element.12), channel_id=1, source_target_pairs={{0,32},{16,48},{32,64},{48,80},{64,96},{80,112},{96,0},{112,16},{1... | collective-permute-start | bytes 1277960 | tf_op jit(solution)/shard_map/ppermute | solution.py:281
  116.2 8.9 %copy-start.5 = (bf16[128,3328]{1,0:T(8,128)(2,1)}, bf16[128,3328]{1,0:T(8,128)(2,1)S(1)}, u32[]{:S(2)}) copy-start(bf16[128,3328]{1,0:T(8,128)(2,1)S(1)} %collective-permute-done.11.refs_4_) | copy-start | bytes 2555908
  116.2 18.3 %collective-permute-start.6 = (bf16[64,3328]{1,0:T(8,128)(2,1)S(1)}, bf16[64,3328]{1,0:T(8,128)(2,1)S(1)}, u32[]{:S(2)}, u32[]{:S(2)}) collective-permute-start(bf16[64,3328]{1,0:T(8,128)(2,1)S(1)} %slice.44), channel_id=1, source_target_pairs={{0,96},{16,112},{32,0},{48,16},{64,32},{80,48},{96,64},{112,80},{1... | collective-permute-start | bytes 1277960 | tf_op jit(solution)/shard_map/ppermute | solution.py:281
  125.0 18.1 %collective-permute-start.8 = (bf16[64,3328]{1,0:T(8,128)(2,1)}, bf16[64,3328]{1,0:T(8,128)(2,1)S(1)}, u32[]{:S(2)}, u32[]{:S(2)}) collective-permute-start(bf16[64,3328]{1,0:T(8,128)(2,1)} %collective-permute-done.5.refs_8_), channel_id=1, source_target_pairs={{0,32},{16,48},{32,64},{48,80},{64,96},{80,112},{96,0},{112,16},{1... | collective-permute-start | bytes 1277960 | tf_op jit(solution)/shard_map/ppermute | solution.py:281
  129.3 49.3 %collective-permute-start.12 = (bf16[64,3328]{1,0:T(8,128)(2,1)}, bf16[64,3328]{1,0:T(8,128)(2,1)}, u32[]{:S(2)}, u32[]{:S(2)}) collective-permute-start(bf16[64,3328]{1,0:T(8,128)(2,1)} %slice.46), channel_id=1, source_target_pairs={{0,32},{16,48},{32,64},{48,80},{64,96},{80,112},{96,0},{112,16},{1... | collective-permute-start | bytes 1277960 | tf_op jit(solution)/shard_map/ppermute | solution.py:281
  134.2 10.6 %copy-start.7 = (bf16[64,3328]{1,0:T(8,128)(2,1)}, bf16[64,3328]{1,0:T(8,128)(2,1)S(1)}, u32[]{:S(2)}) copy-start(bf16[64,3328]{1,0:T(8,128)(2,1)S(1)} %collective-permute-done.2.refs_5_) | copy-start | bytes 1277956
  134.2 44.4 %collective-permute-start.13 = (bf16[64,3328]{1,0:T(8,128)(2,1)}, bf16[64,3328]{1,0:T(8,128)(2,1)}, u32[]{:S(2)}, u32[]{:S(2)}) collective-permute-start(bf16[64,3328]{1,0:T(8,128)(2,1)} %slice.47), channel_id=1, source_target_pairs={{0,96},{16,112},{32,0},{48,16},{64,32},{80,48},{96,64},{112,80},{1... | collective-permute-start | bytes 1277960 | tf_op jit(solution)/shard_map/ppermute | solution.py:281
  134.5 10.3 %copy-start.8 = (bf16[64,3328]{1,0:T(8,128)(2,1)}, bf16[64,3328]{1,0:T(8,128)(2,1)S(1)}, u32[]{:S(2)}) copy-start(bf16[64,3328]{1,0:T(8,128)(2,1)S(1)} %collective-permute-done.6.refs_9_) | copy-start | bytes 1277956
  134.5 37.7 %collective-permute-start.15 = (bf16[128,3328]{1,0:T(8,128)(2,1)}, bf16[128,3328]{1,0:T(8,128)(2,1)}, u32[]{:S(2)}, u32[]{:S(2)}) collective-permute-start(bf16[128,3328]{1,0:T(8,128)(2,1)} %copy-done.6), channel_id=1, source_target_pairs={{0,32},{16,48},{32,64},{48,80},{64,96},{80,112},{96,0},{112,16},{1... | collective-permute-start | bytes 2555912 | tf_op jit(solution)/shard_map/ppermute | solution.py:281
  143.2 13.8 %copy-start.3 = (bf16[64,3328]{1,0:T(8,128)(2,1)}, bf16[64,3328]{1,0:T(8,128)(2,1)S(1)}, u32[]{:S(2)}) copy-start(bf16[64,3328]{1,0:T(8,128)(2,1)S(1)} %collective-permute-done.8.low_ref) | copy-start | bytes 1277956
  143.2 32.1 %collective-permute-start.16 = (bf16[128,3328]{1,0:T(8,128)(2,1)}, bf16[128,3328]{1,0:T(8,128)(2,1)}, u32[]{:S(2)}, u32[]{:S(2)}) collective-permute-start(bf16[128,3328]{1,0:T(8,128)(2,1)} %copy-done.6), channel_id=1, source_target_pairs={{0,96},{16,112},{32,0},{48,16},{64,32},{80,48},{96,64},{112,80},{1... | collective-permute-start | bytes 2555912 | tf_op jit(solution)/shard_map/ppermute | solution.py:281
  143.5 13.4 %collective-permute-start.9 = (bf16[64,3328]{1,0:T(8,128)(2,1)}, bf16[64,3328]{1,0:T(8,128)(2,1)}, u32[]{:S(2)}, u32[]{:S(2)}) collective-permute-start(bf16[64,3328]{1,0:T(8,128)(2,1)} %collective-permute-done.3.refs_6_), channel_id=1, source_target_pairs={{0,16},{16,0},{32,48},{48,32},{64,80},{80,64},{96,112},{112,96},{1... | collective-permute-start | bytes 1277960 | tf_op jit(solution)/shard_map/ppermute | solution.py:287
  162.4 38.1 %all-to-all-start.2 = ((bf16[16,64,1024]{2,1,0:T(8,128)(2,1)}), bf16[16,64,1024]{2,1,0:T(8,128)(2,1)}, u32[]{:S(2)}, u32[]{:S(2)}) async-start(bf16[16,64,1024]{2,1,0:T(8,128)(2,1)} %bitcast.15), calls=%async_computation.2 | async-start | bytes 4194304 | tf_op jit(solution)/shard_map/all_to_all | solution.py:291
  174.1 16.7 %collective-permute-start.17 = (bf16[64,3328]{1,0:T(8,128)(2,1)}, bf16[64,3328]{1,0:T(8,128)(2,1)}, u32[]{:S(2)}, u32[]{:S(2)}) collective-permute-start(bf16[64,3328]{1,0:T(8,128)(2,1)} %slice.48), channel_id=1, source_target_pairs={{0,32},{16,48},{32,64},{48,80},{64,96},{80,112},{96,0},{112,16},{1... | collective-permute-start | bytes 1277960 | tf_op jit(solution)/shard_map/ppermute | solution.py:281
  177.1 13.7 %collective-permute-start.18 = (bf16[64,3328]{1,0:T(8,128)(2,1)}, bf16[64,3328]{1,0:T(8,128)(2,1)}, u32[]{:S(2)}, u32[]{:S(2)}) collective-permute-start(bf16[64,3328]{1,0:T(8,128)(2,1)} %slice.49), channel_id=1, source_target_pairs={{0,96},{16,112},{32,0},{48,16},{64,32},{80,48},{96,64},{112,80},{1... | collective-permute-start | bytes 1277960 | tf_op jit(solution)/shard_map/ppermute | solution.py:281
  200.5 33.9 %all-to-all-start.4 = ((bf16[16,64,1024]{2,1,0:T(8,128)(2,1)}), bf16[16,64,1024]{2,1,0:T(8,128)(2,1)S(1)}, u32[]{:S(2)}, u32[]{:S(2)}) async-start(bf16[16,64,1024]{2,1,0:T(8,128)(2,1)} %bitcast.14), calls=%async_computation.4 | async-start | bytes 4194304 | tf_op jit(solution)/shard_map/all_to_all | solution.py:291

commit v3 on v2

--- a/solution.py
+++ b/solution.py
@@ -95,12 +95,12 @@
     return parts
 
 
-def rotate_kernel(share, scaling, rows_ref, matrix_ref, out_ref, total_ref, columns_ref, arrived):
+def rotate_kernel(share, begin, scaling, raw_ref, matrix_ref, out_ref, total_ref, columns_ref, arrived):
     half = matrix_ref.shape[0]
-    starts = list(range(0, half, 256))
+    starts = list(range(0, half, 512))
     copies = []
     for index, start in enumerate(starts):
-        window = pl.ds(start, min(256, half - start))
+        window = pl.ds(start, min(512, half - start))
         copies.append(
             pltpu.make_async_copy(
                 matrix_ref.at[:, window], columns_ref.at[:, window], arrived.at[index]
@@ -108,13 +108,14 @@
         )
     for copy in copies:
         copy.start()
-    stacked = jnp.concatenate([rows_ref[:, :half], rows_ref[:, half:]], axis=0)
+    rows = raw_ref[:, begin : begin + share, :].reshape(-1, 2 * half)
+    stacked = jnp.concatenate([rows[:, :half], rows[:, half:]], axis=0)
     for index, start in enumerate(starts):
-        width = min(256, half - start)
+        width = min(512, half - start)
         copies[index].wait()
         columns = columns_ref[:, start : start + width]
         total_ref[:, :width] = jnp.dot(stacked, columns, preferred_element_type=jnp.float32)
-        count = rows_ref.shape[0]
+        count = rows.shape[0]
         for lane in range(0, width, 128):
             low, high = (
                 [
@@ -130,21 +131,21 @@
                 out_ref[at, :, other] = ((one - two) * scaling).astype(jnp.bfloat16)
 
 
-def rotate(raw, matrix):
-    groups, share, width = raw.shape
+def rotate(raw, matrix, begin, share):
+    groups, _, width = raw.shape
     scaling = 1.0 / math.sqrt(groups * width)
     return pl.pallas_call(
-        lambda *refs: rotate_kernel(share, scaling, *refs),
-        out_shape=jax.ShapeDtypeStruct(raw.shape, jnp.bfloat16),
+        lambda *refs: rotate_kernel(share, begin, scaling, *refs),
+        out_shape=jax.ShapeDtypeStruct((groups, share, width), jnp.bfloat16),
         in_specs=[
             pl.BlockSpec(memory_space=pltpu.VMEM),
             pl.BlockSpec(memory_space=pl.ANY),
         ],
         out_specs=pl.BlockSpec(memory_space=pltpu.VMEM),
         scratch_shapes=[
-            pltpu.VMEM((2 * groups * share, 256), jnp.float32),
+            pltpu.VMEM((2 * groups * share, 512), jnp.float32),
             pltpu.VMEM(matrix.shape, jnp.bfloat16),
-            pltpu.SemaphoreType.DMA((-(-matrix.shape[0] // 256),)),
+            pltpu.SemaphoreType.DMA((-(-matrix.shape[0] // 512),)),
         ],
         compiler_params=pltpu.CompilerParams(vmem_limit_bytes=56 * 1024 * 1024),
         cost_estimate=pl.CostEstimate(
@@ -152,7 +153,7 @@
             bytes_accessed=width * width // 2 + 4 * groups * share * width,
             transcendentals=0,
         ),
-    )(raw.reshape(groups * share, width), matrix)
+    )(raw, matrix)
 
 
 def block_of(place_ref, shift):
@@ -246,7 +247,7 @@
 
 def product_last(place, weight, before, low, high):
     width, columns = weight.shape
-    tile = 256
+    tile = 512
     rows = 2 * low.shape[0]
     return pl.pallas_call(
         last_kernel,
@@ -275,6 +276,163 @@
     )(place, weight, before, low, high)
 
 
+def split_product_kernel(spec, shifts, place_ref, weight_ref, *refs):
+    pieces = refs[:-4]
+    keep_ref, send_ref, rows_ref, arrived = refs[-4:]
+    blocks, n_rows, width = rows_ref.shape
+
+    @pl.when(pl.program_id(0) == 0)
+    def _():
+        copies = []
+        for index, (source, begin, count, block, start) in enumerate(spec):
+            window = rows_ref.at[block, pl.ds(start, count)]
+            block_rows = pieces[source].at[pl.ds(begin, count)]
+            copies.append(pltpu.make_async_copy(block_rows, window, arrived.at[index]))
+        for copy in copies:
+            copy.start()
+        for copy in copies:
+            copy.wait()
+
+    total = jnp.dot(
+        rows_ref[...].reshape(blocks * n_rows, width),
+        weight_ref[...],
+        preferred_element_type=jnp.float32,
+    ).reshape(blocks, 2, n_rows // 2, weight_ref.shape[1])
+    second = place_ref[2] == 1
+    for block, shift in enumerate(shifts):
+        where = block_of(place_ref, shift)
+        low, high = total[block, 0], total[block, 1]
+        keep_ref[where] = jnp.where(second, high, low)
+        send_ref[where] = jnp.where(second, low, high).astype(jnp.bfloat16)
+
+
+def split_product(place, weight, spec, pieces):
+    width, columns = weight.shape
+    tile = 256
+    blocks = 7
+    rows = sum(count for _, _, count, _, _ in spec) // blocks
+    shifts = [(0, 0), (3, 0), (1, 0), (2, 0), (0, 1), (3, 1), (1, 1)]
+    shape = (blocks + 1, rows // 2, columns)
+    block = pl.BlockSpec((blocks + 1, rows // 2, tile), lambda i: (0, 0, i))
+    return pl.pallas_call(
+        lambda *refs: split_product_kernel(spec, shifts, *refs),
+        grid=(columns // tile,),
+        out_shape=[
+            jax.ShapeDtypeStruct(shape, jnp.float32),
+            jax.ShapeDtypeStruct(shape, jnp.bfloat16),
+        ],
+        in_specs=[
+            pl.BlockSpec(memory_space=pltpu.SMEM),
+            pl.BlockSpec((width, tile), lambda i: (0, i)),
+        ]
+        + [pl.BlockSpec(memory_space=pl.ANY)] * len(pieces),
+        out_specs=[block, block],
+        scratch_shapes=[
+            pltpu.VMEM((blocks, rows, width), jnp.bfloat16),
+            pltpu.SemaphoreType.DMA((len(spec),)),
+        ],
+        compiler_params=pltpu.CompilerParams(vmem_limit_bytes=56 * 1024 * 1024),
+        cost_estimate=pl.CostEstimate(
+            flops=50 * blocks * rows * width * columns,
+            bytes_accessed=2 * (width * columns + blocks * rows * (width + columns)),
+            transcendentals=0,
+        ),
+    )(place, weight, *pieces)
+
+
+def split_last_kernel(
+    place_ref, weight_ref, kept, sent, low_ref, high_ref, keep_ref, send_ref, rows_ref, keeps_ref, sends_ref, arrived
+):
+    step = pl.program_id(0)
+    steps, half, tile = keeps_ref.shape
+
+    @pl.when(step == 0)
+    def _():
+        rows_ref[:half] = low_ref[...]
+        rows_ref[half:] = high_ref[...]
+
+    total = jnp.dot(rows_ref[...], weight_ref[...], preferred_element_type=jnp.float32)
+    second = place_ref[2] == 1
+    low, high = total[:half], total[half:]
+    keeps_ref[step] = jnp.where(second, high, low)
+    sends_ref[step] = jnp.where(second, low, high).astype(jnp.bfloat16)
+
+    @pl.when(step == steps - 1)
+    def _():
+        copies = []
+        where = block_of(place_ref, (2, 1))
+        for index in range(steps):
+            window = pl.ds(index * tile, tile)
+            for side, (part_ref, out_ref) in enumerate(((keeps_ref, keep_ref), (sends_ref, send_ref))):
+                copies.append(
+                    pltpu.make_async_copy(
+                        part_ref.at[index], out_ref.at[where, :, window], arrived.at[side, index]
+                    )
+                )
+        for copy in copies:
+            copy.start()
+        for copy in copies:
+            copy.wait()
+
+
+def split_product_last(place, weight, kept, sent, arrived_rows):
+    width, columns = weight.shape
+    tile = 512
+    half = arrived_rows.shape[0] // 2
+    steps = columns // tile
+    return pl.pallas_call(
+        split_last_kernel,
+        grid=(steps,),
+        out_shape=[
+            jax.ShapeDtypeStruct(kept.shape, jnp.float32),
+            jax.ShapeDtypeStruct(sent.shape, jnp.bfloat16),
+        ],
+        in_specs=[
+            pl.BlockSpec(memory_space=pltpu.SMEM),
+            pl.BlockSpec((width, tile), lambda i: (0, i)),
+            pl.BlockSpec(memory_space=pl.ANY),
+            pl.BlockSpec(memory_space=pl.ANY),
+            pl.BlockSpec((half, width), lambda i: (0, 0)),
+            pl.BlockSpec((half, width), lambda i: (1, 0)),
+        ],
+        out_specs=[pl.BlockSpec(memory_space=pl.ANY)] * 2,
+        scratch_shapes=[
+            pltpu.VMEM((2 * half, width), jnp.bfloat16),
+            pltpu.VMEM((steps, half, tile), jnp.float32),
+            pltpu.VMEM((steps, half, tile), jnp.bfloat16),
+            pltpu.SemaphoreType.DMA((2, steps)),
+        ],
+        input_output_aliases={2: 0, 3: 1},
+        compiler_params=pltpu.CompilerParams(vmem_limit_bytes=56 * 1024 * 1024),
+        cost_estimate=pl.CostEstimate(
+            flops=4 * half * width * columns,
+            bytes_accessed=2 * (width * columns + 2 * half * (width + columns)),
+            transcendentals=0,
+        ),
+    )(place, weight, kept, sent, arrived_rows, arrived_rows)
+
+
+def total_kernel(keep_ref, got_ref, out_ref):
+    out_ref[...] = (keep_ref[...] + got_ref[...].astype(jnp.float32)).astype(jnp.bfloat16)
+
+
+def reduce_shares(keep, send):
+    count = lax.axis_size("tp")
+    got = lax.ppermute(send, "tp", [(i, i ^ 1) for i in range(count)])
+    blocks, rows, columns = keep.shape
+    spec = pl.BlockSpec((blocks // 4, rows, columns), lambda i: (i, 0, 0))
+    total = pl.pallas_call(
+        total_kernel,
+        grid=(4,),
+        out_shape=jax.ShapeDtypeStruct(keep.shape, jnp.bfloat16),
+        in_specs=[spec, spec],
+        out_specs=spec,
+    )(keep, got)
+    groups = [list(range(core, count, 2)) for core in range(2)]
+    parts = lax.all_to_all(total, "tp", 0, 0, axis_index_groups=groups, tiled=True)
+    return jnp.sum(parts.astype(jnp.float32), axis=0)
+
+
 def ring(step):
     def move(block):
         count = lax.axis_size("ctx")
@@ -306,15 +464,19 @@
     matrix = jnp.asarray(np.kron(sylvester(width // 104), paley_matrix()), jnp.bfloat16)
     flips = (1 - 2 * sign_bits).astype(jnp.bfloat16)
     ctx = lax.axis_index("ctx")
-    place = jnp.stack([ctx // 2, ctx % 2]).astype(jnp.int32)
+    place = jnp.stack([ctx // 2, ctx % 2, lax.axis_index("tp") % 2]).astype(jnp.int32)
     up, down = ring(1), ring(-1)
     rows = tokens // 2
     half, quarter = rows // 2, rows // 4
-    got = exchange((hidden * flips).reshape(groups, 2 * share, width))
+    cut = hidden.reshape(groups, 2, share, width)
+    raw0, raw1 = cut[:, 0] * flips, cut[:, 1] * flips
+    got = exchange(raw0)
     weight = decode_weights(weight_codes, weight_exps)
-    got, weight = sync(got, weight)
-    own0 = exchange(rotate(got[:, :share], matrix)).reshape(rows, width)
-    rotated1 = rotate(got[:, share:], matrix)
+    got, weight, raw1 = sync(got, weight, raw1)
+    own0 = exchange(rotate(got, matrix, 0, share)).reshape(rows, width)
+    raw1, own0 = sync(raw1, own0)
+    got1 = exchange(raw1)
+    rotated1 = rotate(got1, matrix, 0, share)
     own0, rotated1, weight = keep(own0, rotated1, weight)
 
     below0, above0, other0 = up(own0), down(own0), across(own0)
@@ -322,26 +484,16 @@
     below0, above0, other0, own1, weight = keep(below0, above0, other0, own1, weight)
 
     other_below0, other_above0 = up(other0[:half]), down(other0[:half])
-    far0 = [up(below0[:half]), down(above0[half:])]
+    far0 = [up(below0)]
     late0 = across(jnp.concatenate([below0[half:], above0[half:]]))
     other_below0, other_above0, late0, own1, *far0 = keep(
         other_below0, other_above0, late0, own1, *far0
     )
 
-    spec = [
-        (0, 0, rows, 0, 0),
-        (1, 0, rows, 1, 0),
-        (2, 0, rows, 2, 0),
-        (3, 0, half, 3, 0),
-        (4, 0, half, 3, half),
-        (5, 0, rows, 4, 0),
-        (6, 0, half, 5, 0),
-        (7, 0, half, 6, 0),
-        (8, 0, half, 5, half),
-        (8, half, half, 6, half),
-    ]
-    last0 = up(other_below0)
-    late_far0 = across(far0[1])
+    spec = [(index, 0, rows, index, 0) for index in range(5)]
+    spec += [(5, 0, half, 5, 0), (6, 0, half, 6, 0), (7, 0, half, 5, half), (7, half, half, 6, half)]
+    last0 = down(other_above0)
+    late_far0 = across(far0[0][half:])
     below1, above1, other1 = up(own1), down(own1), across(own1)
     pieces0 = [own0, below0, above0, *far0, other0, other_below0, other_above0, late0]
     part0 = product(place, weight, spec, pieces0)
@@ -352,21 +504,17 @@
     part0 = product_last(place, weight, part0, last0, late_far0)
     sent0 = exchange(part0.reshape(groups, half, columns))
     other_below1, other_above1 = up(other1), down(other1)
-    far1 = [up(below1[:half]), down(above1[half:])]
+    far1 = [down(above1)]
     other_below1, other_above1, *far1 = keep(other_below1, other_above1, *far1)
 
-    last1 = [up(other_below1[:half]), down(other_above1[half:])]
-    spec1 = [(0, 0, rows, 0, 0), (1, 0, rows, 1, 0), (2, 0, rows, 2, 0), (3, 0, half, 3, 0)]
-    spec1 += [(4, 0, half, 3, half), (5, 0, rows, 4, 0), (6, 0, rows, 5, 0), (7, 0, rows, 6, 0)]
+    last1 = [up(other_below1)]
+    spec1 = [(index, 0, rows, index, 0) for index in range(7)]
     pieces1 = [own1, below1, above1, *far1, other1, other_below1, other_above1]
-    part1 = product(place, weight, spec1, pieces1)
-    part1, *last1 = keep(part1, *last1)
-    part1 = product_last(place, weight, part1, *last1)
-    sent1 = exchange(part1.reshape(groups, half, columns))
-    outs = [
-        jnp.sum(sent.astype(jnp.float32), axis=0).reshape(groups // 2, share, columns)
-        for sent in (sent0, sent1)
-    ]
+    kept, sent = split_product(place, weight, spec1, pieces1)
+    kept, sent = split_product_last(place, weight, kept, sent, *last1)
+    out1 = reduce_shares(kept, sent)
+    out0 = jnp.sum(sent0.astype(jnp.float32), axis=0)
+    outs = [out.reshape(groups // 2, share, columns) for out in (out0, out1)]
     return jnp.concatenate(outs, axis=1).reshape(rows, columns)
 
 

time: 237 us -> 220 us (0.928)
  waiting for transfers between devices: 82.4 us -> 69.2 us
  local copies, waits for them, and re-layouts: 11.5 us -> 6.76 us
    all_to_all x4, waiting for transfers between devices: 53.5 us -> 13.1 us  [exchange(): return lax.all_to_all(block, 'tp', 0, 0, tiled=True)]
    pallas_call x2 -> x5, Pallas kernels: 15.3 us -> 32.9 us  [the longest x1 12.3 us: split_product(): pl.pallas_call(lambda *refs: split_product_kernel(spec, shifts, *refs), g...]
    all_to_all x0 -> x1, waiting for transfers between devices: none -> 12.9 us  [reduce_shares(): lax.all_to_all(total, 'tp', 0, 0, axis_index_groups=groups, tiled=True)]
    pallas_call x2 -> x1, Pallas kernels: 24.3 us -> 12.1 us  [product(): pl.pallas_call(lambda *refs: product_kernel(spec, shifts, *refs), grid=(c...]
    ppermute x15 -> x12, waiting for transfers between devices: 17.5 us -> 25.6 us  [move(): lax.ppermute(block, 'ctx', [(i, (i + 2 * step) % count) for i in range(co...]
    slice x5 -> x1, local copies, waits for them, and re-layouts: 8.22 us -> 1.78 us  [shards(): late_far0 = across(far0[0][half:])]
    pallas_call x2 -> x1, Pallas kernels: 10.8 us -> 4.63 us  [product_last(): pl.pallas_call(last_kernel, grid=(columns // tile,), out_shape=jax.ShapeD...]
    all_to_all x0 -> x1, starting transfers between devices: none -> 4.33 us  [reduce_shares(): lax.all_to_all(total, 'tp', 0, 0, axis_index_groups=groups, tiled=True)]
  transfers between devices with their start and end apart: 23 -> 22, of which waited for: 8 -> 10; matrix products, arithmetic and copies ran while one was open for 5% -> 3% of each run, Pallas kernels for 24% -> 26%
where the time goes in v3:
time: 220 us; the launch traced here: 219 us
  waiting for transfers between devices  69.2 us (31%)
  Pallas kernels  64 us (29%)
  starting transfers between devices  52.3 us (24%)
  blocking collectives  19 us (9%)
  other arithmetic  7.15 us (3%)
  local copies, waits for them, and re-layouts  6.76 us (3%)
    all_to_all x4, starting transfers between devices, exchange(): return lax.all_to_all(block, 'tp', 0, 0, tiled=True)  27.5 us
    ppermute x12, waiting for transfers between devices, move(): lax.ppermute(block, 'ctx', [(i, (i + 2 * step) % count) for i in range(co...  25.6 us
    all_to_all x1, blocking collectives, exchange(): return lax.all_to_all(block, 'tp', 0, 0, tiled=True)  19 us
    ppermute x4, waiting for transfers between devices, across(): lax.ppermute(block, 'ctx', [(i, i ^ 1) for i in range(lax.axis_size('ctx'...  15 us
    pallas_call x1, Pallas kernels, decode_weights(): pl.pallas_call(decode_kernel, grid=(rows // step,), out_shape=jax.ShapeDt...  14.3 us
    all_to_all x4, waiting for transfers between devices, exchange(): return lax.all_to_all(block, 'tp', 0, 0, tiled=True)  13.1 us
    all_to_all x1, waiting for transfers between devices, reduce_shares(): lax.all_to_all(total, 'tp', 0, 0, axis_index_groups=groups, tiled=True)  12.9 us
    ppermute x12, starting transfers between devices, move(): lax.ppermute(block, 'ctx', [(i, (i + 2 * step) % count) for i in range(co...  12.7 us
  transfers between devices with their start and end apart: 22, of which 10 were waited for; matrix products, arithmetic and copies ran while one was open for 3% of the time, Pallas kernels for 26%

profile of v3, /device:TPU:1, one launch (start us, length us, event | category | flops | bytes accessed | tf_op | source)
XLA Modules:
  0.0 218.6 jit_solution(14189391238181095872)
XLA Ops:
  0.7 2.8 %fusion = (bf16[16,8,3328]{2,1,0:T(8,128)(2,1)}, bf16[16,8,3328]{2,1,0:T(8,128)(2,1)}) fusion(bf16[16,2,8,3328]{3,2,1,0:T(8,128)(2,1)} %bitcast.23, bf16[3328]{0:T(1024)(128)(2,1)S(1)} %subtract_convert_fusion), kind=kLoop, calls=%fused_computation.3 | loop fusion | flops 851968 | bytes 3414528 | tf_op jit(solution)/shard_map/mul | solution.py:472
  3.5 7.8 %all-to-all-start = ((bf16[16,8,3328]{2,1,0:T(8,128)(2,1)}), bf16[16,8,3328]{2,1,0:T(8,128)(2,1)S(1)}, u32[]{:S(2)}, u32[]{:S(2)}) async-start(bf16[16,8,3328]{2,1,0:T(8,128)(2,1)} %get-tuple-element.24), calls=%async_computation | async-start | bytes 1703936 | tf_op jit(solution)/shard_map/all_to_all | solution.py:449
  11.3 14.3 %shard_map.55.refs_1_.weight_ref = bf16[3328,1024]{1,0:T(8,128)(2,1)} custom-call(s32[3328,1024]{1,0:T(8,128)} %codes_ref.1, s32[104,1024]{1,0:T(8,128)} %exps_ref.1), custom_call_target="tpu_custom_call" | custom-call | flops 34078720 | bytes 20447232 | tf_op jit(solution)/shard_map/pallas_call | solution.py:69
  26.6 6.1 %shard_map.56 = bf16[16,8,3328]{2,1,0:T(8,128)(2,1)} custom-call(bf16[16,8,3328]{2,1,0:T(8,128)(2,1)} %copy-done.1, bf16[1664,1664]{1,0:T(8,128)(2,1)} %constant.43.clone.refs_1_), custom_call_target="tpu_custom_call" | custom-call | flops 1417674752 | bytes 7241728 | tf_op jit(solution)/shard_map/pallas_call | solution.py:137
  32.7 19.0 %all_to_all.30 = bf16[16,8,3328]{2,1,0:T(8,128)(2,1)S(1)} all-to-all(bf16[16,8,3328]{2,1,0:T(8,128)(2,1)} %shard_map.56), channel_id=1, replica_groups=mesh['ctx'=8,'tp'=16] {'tp'}, dimensions={0} | all-to-all | bytes 1703936 | tf_op jit(solution)/shard_map/all_to_all | solution.py:449
  51.7 4.6 %all-to-all-start.3 = ((bf16[16,8,3328]{2,1,0:T(8,128)(2,1)}), bf16[16,8,3328]{2,1,0:T(8,128)(2,1)S(1)}, u32[]{:S(2)}, u32[]{:S(2)}) async-start(bf16[16,8,3328]{2,1,0:T(8,128)(2,1)} %get-tuple-element.18), calls=%async_computation.3 | async-start | bytes 1703936 | tf_op jit(solution)/shard_map/all_to_all | solution.py:449
  56.3 2.5 %collective-permute-start.3 = (bf16[128,3328]{1,0:T(8,128)(2,1)S(1)}, bf16[128,3328]{1,0:T(8,128)(2,1)S(1)}, u32[]{:S(2)}, u32[]{:S(2)}) collective-permute-start(bf16[128,3328]{1,0:T(8,128)(2,1)S(1)} %bitcast.26), channel_id=1, source_target_pairs={{0,16},{16,0},{32,48},{48,32},{64,80},{80,64},{96,112},{112,96},{1... | collective-permute-start | bytes 2555912 | tf_op jit(solution)/shard_map/ppermute | solution.py:445
  61.5 8.6 %all-to-all-done.3.refs_0_ = bf16[16,8,3328]{2,1,0:T(8,128)(2,1)S(1)} async-done(((bf16[16,8,3328]{2,1,0:T(8,128)(2,1)}), bf16[16,8,3328]{2,1,0:T(8,128)(2,1)S(1)}, u32[]{:S(2)}, u32[]{:S(2)}) %all-to-all-start.3) | async-done | bytes 852000 | tf_op jit(solution)/shard_map/all_to_all | solution.py:449
  71.0 6.1 %shard_map.59 = bf16[16,8,3328]{2,1,0:T(8,128)(2,1)} custom-call(bf16[16,8,3328]{2,1,0:T(8,128)(2,1)} %copy-done, bf16[1664,1664]{1,0:T(8,128)(2,1)} %constant.43.clone.refs_1_), custom_call_target="tpu_custom_call" | custom-call | flops 1417674752 | bytes 7241728 | tf_op jit(solution)/shard_map/pallas_call | solution.py:137
  77.1 5.4 %all-to-all-start.4 = ((bf16[16,8,3328]{2,1,0:T(8,128)(2,1)}), bf16[16,8,3328]{2,1,0:T(8,128)(2,1)}, u32[]{:S(2)}, u32[]{:S(2)}) async-start(bf16[16,8,3328]{2,1,0:T(8,128)(2,1)} %shard_map.59), calls=%async_computation.4 | async-start | bytes 1703936 | tf_op jit(solution)/shard_map/all_to_all | solution.py:449
  82.5 4.9 %collective-permute-done.3.refs_6_ = bf16[128,3328]{1,0:T(8,128)(2,1)S(1)} collective-permute-done((bf16[128,3328]{1,0:T(8,128)(2,1)S(1)}, bf16[128,3328]{1,0:T(8,128)(2,1)S(1)}, u32[]{:S(2)}, u32[]{:S(2)}) %collective-permute-start.3) | collective-permute-done | bytes 852000 | tf_op jit(solution)/shard_map/ppermute | solution.py:445
  87.4 2.8 %collective-permute-start.5 = (bf16[64,3328]{1,0:T(8,128)(2,1)S(1)}, bf16[64,3328]{1,0:T(8,128)(2,1)S(1)}, u32[]{:S(2)}, u32[]{:S(2)}) collective-permute-start(bf16[64,3328]{1,0:T(8,128)(2,1)S(1)} %slice.27), channel_id=1, source_target_pairs={{0,96},{16,112},{32,0},{48,16},{64,32},{80,48},{96,64},{112,80},{1... | collective-permute-start | bytes 1277960 | tf_op jit(solution)/shard_map/ppermute | solution.py:439
  93.1 4.6 %all-to-all-done.4 = bf16[16,8,3328]{2,1,0:T(8,128)(2,1)} async-done(((bf16[16,8,3328]{2,1,0:T(8,128)(2,1)}), bf16[16,8,3328]{2,1,0:T(8,128)(2,1)}, u32[]{:S(2)}, u32[]{:S(2)}) %all-to-all-start.4) | async-done | bytes 852000 | tf_op jit(solution)/shard_map/all_to_all | solution.py:449
  97.6 2.5 %collective-permute-start.12 = (bf16[128,3328]{1,0:T(8,128)(2,1)}, bf16[128,3328]{1,0:T(8,128)(2,1)}, u32[]{:S(2)}, u32[]{:S(2)}) collective-permute-start(bf16[128,3328]{1,0:T(8,128)(2,1)} %bitcast.9.refs_2_), channel_id=1, source_target_pairs={{0,16},{16,0},{32,48},{48,32},{64,80},{80,64},{96,112},{112,96},{1... | collective-permute-start | bytes 2555912 | tf_op jit(solution)/shard_map/ppermute | solution.py:445
  100.1 2.7 %collective-permute-start.10 = (bf16[128,3328]{1,0:T(8,128)(2,1)}, bf16[128,3328]{1,0:T(8,128)(2,1)}, u32[]{:S(2)}, u32[]{:S(2)}) collective-permute-start(bf16[128,3328]{1,0:T(8,128)(2,1)} %bitcast.9.refs_2_), channel_id=1, source_target_pairs={{0,96},{16,112},{32,0},{48,16},{64,32},{80,48},{96,64},{112,80},{1... | collective-permute-start | bytes 2555912 | tf_op jit(solution)/shard_map/ppermute | solution.py:439
  102.8 9.2 %collective-permute-done.2.refs_5_ = bf16[128,3328]{1,0:T(8,128)(2,1)} collective-permute-done((bf16[128,3328]{1,0:T(8,128)(2,1)}, bf16[128,3328]{1,0:T(8,128)(2,1)}, u32[]{:S(2)}, u32[]{:S(2)}) %collective-permute-start.2) | collective-permute-done | bytes 852000 | tf_op jit(solution)/shard_map/ppermute | solution.py:439
  112.6 1.8 slice.30
  114.4 6.8 %collective-permute-done.4.refs_7_ = bf16[64,3328]{1,0:T(8,128)(2,1)S(1)} collective-permute-done((bf16[64,3328]{1,0:T(8,128)(2,1)S(1)}, bf16[64,3328]{1,0:T(8,128)(2,1)S(1)}, u32[]{:S(2)}, u32[]{:S(2)}) %collective-permute-start.4) | collective-permute-done | bytes 426016 | tf_op jit(solution)/shard_map/ppermute | solution.py:439
  121.6 10.1 %collective-permute-done.12.refs_6_ = bf16[128,3328]{1,0:T(8,128)(2,1)} collective-permute-done((bf16[128,3328]{1,0:T(8,128)(2,1)}, bf16[128,3328]{1,0:T(8,128)(2,1)}, u32[]{:S(2)}, u32[]{:S(2)}) %collective-permute-start.12) | collective-permute-done | bytes 852000 | tf_op jit(solution)/shard_map/ppermute | solution.py:445
  131.8 2.3 %collective-permute-start.13 = (bf16[128,3328]{1,0:T(8,128)(2,1)}, bf16[128,3328]{1,0:T(8,128)(2,1)}, u32[]{:S(2)}, u32[]{:S(2)}) collective-permute-start(bf16[128,3328]{1,0:T(8,128)(2,1)} %collective-permute-done.12.refs_6_), channel_id=1, source_target_pairs={{0,32},{16,48},{32,64},{48,80},{64,96},{80,112},{96,0},{112,16},{1... | collective-permute-start | bytes 2555912 | tf_op jit(solution)/shard_map/ppermute | solution.py:439
  136.1 12.1 %shard_map.57.before_ref = bf16[8,128,1024]{2,1,0:T(8,128)(2,1)} custom-call(s32[3]{0:T(128)} %pad_add_fusion.refs_0_.place_ref, bf16[3328,1024]{1,0:T(8,128)(2,1)} %shard_map.55.refs_1_.weight_ref, bf16[128,3328]{1,0:T(8,128)(2,1)} %bitcast.29, bf16[128,3328]{1,0:T(8,128)(2,1)} %collective-permute-done.refs_3_, ...), custom_call_target="tpu_custom_call" | custom-call | flops 152672665600 | bytes 14614528 | tf_op jit(solution)/shard_map/pallas_call | solution.py:199
  148.2 4.6 %shard_map.58 = bf16[8,128,1024]{2,1,0:T(8,128)(2,1)} custom-call(s32[3]{0:T(128)} %pad_add_fusion.refs_0_.place_ref, bf16[3328,1024]{1,0:T(8,128)(2,1)} %shard_map.55.refs_1_.weight_ref, bf16[8,128,1024]{2,1,0:T(8,128)(2,1)} %shard_map.57.before_ref, bf16[64,3328]{1,0:T(8,128)(2,1)} %copy-done.4, ...), custom_call_target="tpu_custom_call", output_to_operand_aliasing={{}: (2, {})} | custom-call | flops 872415232 | bytes 7929856 | tf_op jit(solution)/shard_map/pallas_call | solution.py:252
  152.9 9.7 %all-to-all-start.2 = ((bf16[16,64,1024]{2,1,0:T(8,128)(2,1)}), bf16[16,64,1024]{2,1,0:T(8,128)(2,1)}, u32[]{:S(2)}, u32[]{:S(2)}) async-start(bf16[16,64,1024]{2,1,0:T(8,128)(2,1)} %bitcast.22), calls=%async_computation.2 | async-start | bytes 4194304 | tf_op jit(solution)/shard_map/all_to_all | solution.py:449
  162.7 8.3 %collective-permute-done.11.refs_5_ = bf16[128,3328]{1,0:T(8,128)(2,1)} collective-permute-done((bf16[128,3328]{1,0:T(8,128)(2,1)}, bf16[128,3328]{1,0:T(8,128)(2,1)}, u32[]{:S(2)}, u32[]{:S(2)}) %collective-permute-start.11) | collective-permute-done | bytes 852000 | tf_op jit(solution)/shard_map/ppermute | solution.py:439
  171.0 12.3 %shard_map.60 = (f32[8,64,1024]{2,1,0:T(8,128)}, bf16[8,64,1024]{2,1,0:T(8,128)(2,1)}) custom-call(s32[3]{0:T(128)} %pad_add_fusion.refs_0_.place_ref, bf16[3328,1024]{1,0:T(8,128)(2,1)} %shard_map.55.refs_1_.weight_ref, bf16[128,3328]{1,0:T(8,128)(2,1)} %bitcast.9.refs_2_, bf16[128,3328]{1,0:T(8,128)(2,1)} %collective-permute-done.9.refs_3_, ...), custom_call_target="tpu_custom_call" | custom-call | flops 152672665600 | bytes 14614528 | tf_op jit(solution)/shard_map/pallas_call | solution.py:317
  184.6 4.7 %shard_map.61 = (f32[8,64,1024]{2,1,0:T(8,128)}, bf16[8,64,1024]{2,1,0:T(8,128)(2,1)}) custom-call(s32[3]{0:T(128)} %pad_add_fusion.refs_0_.place_ref, bf16[3328,1024]{1,0:T(8,128)(2,1)} %shard_map.55.refs_1_.weight_ref, f32[8,64,1024]{2,1,0:T(8,128)} %get-tuple-element.19.kept, ...), custom_call_target="tpu_custom_call", output_to_operand_aliasing={{0}: (2, {}), {1}: (3, {})} | custom-call | flops 872415232 | bytes 7929856 | tf_op jit(solution)/shard_map/pallas_call | solution.py:383
  189.3 1.8 collective-permute-start.16
  191.1 2.5 %collective-permute-done.16.got_ref = bf16[8,64,1024]{2,1,0:T(8,128)(2,1)S(1)} collective-permute-done((bf16[8,64,1024]{2,1,0:T(8,128)(2,1)}, bf16[8,64,1024]{2,1,0:T(8,128)(2,1)S(1)}, u32[]{:S(2)}, u32[]{:S(2)}) %collective-permute-start.16) | collective-permute-done | bytes 1048608 | tf_op jit(solution)/shard_map/ppermute | solution.py:421
  194.6 3.8 %shard_map.62 = bf16[8,64,1024]{2,1,0:T(8,128)(2,1)} custom-call(f32[8,64,1024]{2,1,0:T(8,128)} %get-tuple-element.21.keep_ref, bf16[8,64,1024]{2,1,0:T(8,128)(2,1)} %copy-done.2), custom_call_target="tpu_custom_call" | custom-call | tf_op jit(solution)/shard_map/pallas_call | solution.py:424
  198.3 4.3 %all-to-all-start.5 = ((bf16[8,64,1024]{2,1,0:T(8,128)(2,1)}), bf16[8,64,1024]{2,1,0:T(8,128)(2,1)S(1)}, u32[]{:S(2)}, u32[]{:S(2)}) async-start(bf16[8,64,1024]{2,1,0:T(8,128)(2,1)} %shard_map.62), calls=%async_computation.5 | async-start | bytes 2097152 | tf_op jit(solution)/shard_map/all_to_all | solution.py:432
  202.7 2.0 convert_reduce_fusion
  204.7 12.9 %all-to-all-done.5 = bf16[8,64,1024]{2,1,0:T(8,128)(2,1)S(1)} async-done(((bf16[8,64,1024]{2,1,0:T(8,128)(2,1)}), bf16[8,64,1024]{2,1,0:T(8,128)(2,1)S(1)}, u32[]{:S(2)}, u32[]{:S(2)}) %all-to-all-start.5) | async-done | bytes 1048608 | tf_op jit(solution)/shard_map/all_to_all | solution.py:432
  (48 shorter events, 14.6 us)
Async XLA Ops:
  3.5 22.0 %all-to-all-start = ((bf16[16,8,3328]{2,1,0:T(8,128)(2,1)}), bf16[16,8,3328]{2,1,0:T(8,128)(2,1)S(1)}, u32[]{:S(2)}, u32[]{:S(2)}) async-start(bf16[16,8,3328]{2,1,0:T(8,128)(2,1)} %get-tuple-element.24), calls=%async_computation | async-start | bytes 1703936 | tf_op jit(solution)/shard_map/all_to_all | solution.py:449
  25.6 1.0 copy-start.1
  51.7 25.4 %copy-start.3 = (bf16[16,8,3328]{2,1,0:T(8,128)(2,1)}, bf16[16,8,3328]{2,1,0:T(8,128)(2,1)S(1)}, u32[]{:S(2)}) copy-start(bf16[16,8,3328]{2,1,0:T(8,128)(2,1)S(1)} %all_to_all.30) | copy-start | bytes 2555908
  51.7 18.3 %all-to-all-start.3 = ((bf16[16,8,3328]{2,1,0:T(8,128)(2,1)}), bf16[16,8,3328]{2,1,0:T(8,128)(2,1)S(1)}, u32[]{:S(2)}, u32[]{:S(2)}) async-start(bf16[16,8,3328]{2,1,0:T(8,128)(2,1)} %get-tuple-element.18), calls=%async_computation.3 | async-start | bytes 1703936 | tf_op jit(solution)/shard_map/all_to_all | solution.py:449
  56.3 31.1 %collective-permute-start.3 = (bf16[128,3328]{1,0:T(8,128)(2,1)S(1)}, bf16[128,3328]{1,0:T(8,128)(2,1)S(1)}, u32[]{:S(2)}, u32[]{:S(2)}) collective-permute-start(bf16[128,3328]{1,0:T(8,128)(2,1)S(1)} %bitcast.26), channel_id=1, source_target_pairs={{0,16},{16,0},{32,48},{48,32},{64,80},{80,64},{96,112},{112,96},{1... | collective-permute-start | bytes 2555912 | tf_op jit(solution)/shard_map/ppermute | solution.py:445
  58.8 31.5 %collective-permute-start = (bf16[128,3328]{1,0:T(8,128)(2,1)S(1)}, bf16[128,3328]{1,0:T(8,128)(2,1)}, u32[]{:S(2)}, u32[]{:S(2)}) collective-permute-start(bf16[128,3328]{1,0:T(8,128)(2,1)S(1)} %bitcast.27), channel_id=1, source_target_pairs={{0,32},{16,48},{32,64},{48,80},{64,96},{80,112},{96,0},{112,16},{1... | collective-permute-start | bytes 2555912 | tf_op jit(solution)/shard_map/ppermute | solution.py:439
  60.1 31.3 %collective-permute-start.1 = (bf16[128,3328]{1,0:T(8,128)(2,1)S(1)}, bf16[128,3328]{1,0:T(8,128)(2,1)}, u32[]{:S(2)}, u32[]{:S(2)}) collective-permute-start(bf16[128,3328]{1,0:T(8,128)(2,1)S(1)} %bitcast.28), channel_id=1, source_target_pairs={{0,96},{16,112},{32,0},{48,16},{64,32},{80,48},{96,64},{112,80},{1... | collective-permute-start | bytes 2555912 | tf_op jit(solution)/shard_map/ppermute | solution.py:439
  70.1 0.9 copy-start
  77.1 20.5 %all-to-all-start.4 = ((bf16[16,8,3328]{2,1,0:T(8,128)(2,1)}), bf16[16,8,3328]{2,1,0:T(8,128)(2,1)}, u32[]{:S(2)}, u32[]{:S(2)}) async-start(bf16[16,8,3328]{2,1,0:T(8,128)(2,1)} %shard_map.59), calls=%async_computation.4 | async-start | bytes 1703936 | tf_op jit(solution)/shard_map/all_to_all | solution.py:449
  87.4 5.1 %copy-start.5 = (bf16[128,3328]{1,0:T(8,128)(2,1)}, bf16[128,3328]{1,0:T(8,128)(2,1)S(1)}, u32[]{:S(2)}) copy-start(bf16[128,3328]{1,0:T(8,128)(2,1)S(1)} %collective-permute-done.3.refs_6_) | copy-start | bytes 2555908
  87.4 15.4 %collective-permute-start.5 = (bf16[64,3328]{1,0:T(8,128)(2,1)S(1)}, bf16[64,3328]{1,0:T(8,128)(2,1)S(1)}, u32[]{:S(2)}, u32[]{:S(2)}) collective-permute-start(bf16[64,3328]{1,0:T(8,128)(2,1)S(1)} %slice.27), channel_id=1, source_target_pairs={{0,96},{16,112},{32,0},{48,16},{64,32},{80,48},{96,64},{112,80},{1... | collective-permute-start | bytes 1277960 | tf_op jit(solution)/shard_map/ppermute | solution.py:439
  91.3 20.8 %collective-permute-start.2 = (bf16[128,3328]{1,0:T(8,128)(2,1)}, bf16[128,3328]{1,0:T(8,128)(2,1)}, u32[]{:S(2)}, u32[]{:S(2)}) collective-permute-start(bf16[128,3328]{1,0:T(8,128)(2,1)} %collective-permute-done.refs_3_), channel_id=1, source_target_pairs={{0,32},{16,48},{32,64},{48,80},{64,96},{80,112},{96,0},{112,16},{1... | collective-permute-start | bytes 2555912 | tf_op jit(solution)/shard_map/ppermute | solution.py:439
  92.5 28.7 %collective-permute-start.6 = (bf16[128,3328]{1,0:T(8,128)(2,1)S(1)}, bf16[128,3328]{1,0:T(8,128)(2,1)}, u32[]{:S(2)}, u32[]{:S(2)}) collective-permute-start(bf16[128,3328]{1,0:T(8,128)(2,1)S(1)} %pad_maximum_fusion), channel_id=1, source_target_pairs={{0,16},{16,0},{32,48},{48,32},{64,80},{80,64},{96,112},{112,96},{1... | collective-permute-start | bytes 2555912 | tf_op jit(solution)/shard_map/ppermute | solution.py:445
  97.6 34.1 %collective-permute-start.12 = (bf16[128,3328]{1,0:T(8,128)(2,1)}, bf16[128,3328]{1,0:T(8,128)(2,1)}, u32[]{:S(2)}, u32[]{:S(2)}) collective-permute-start(bf16[128,3328]{1,0:T(8,128)(2,1)} %bitcast.9.refs_2_), channel_id=1, source_target_pairs={{0,16},{16,0},{32,48},{48,32},{64,80},{80,64},{96,112},{112,96},{1... | collective-permute-start | bytes 2555912 | tf_op jit(solution)/shard_map/ppermute | solution.py:445
  100.1 34.4 %collective-permute-start.10 = (bf16[128,3328]{1,0:T(8,128)(2,1)}, bf16[128,3328]{1,0:T(8,128)(2,1)}, u32[]{:S(2)}, u32[]{:S(2)}) collective-permute-start(bf16[128,3328]{1,0:T(8,128)(2,1)} %bitcast.9.refs_2_), channel_id=1, source_target_pairs={{0,96},{16,112},{32,0},{48,16},{64,32},{80,48},{96,64},{112,80},{1... | collective-permute-start | bytes 2555912 | tf_op jit(solution)/shard_map/ppermute | solution.py:439
  102.8 33.3 %copy-start.6 = (bf16[64,3328]{1,0:T(8,128)(2,1)}, bf16[64,3328]{1,0:T(8,128)(2,1)S(1)}, u32[]{:S(2)}) copy-start(bf16[64,3328]{1,0:T(8,128)(2,1)S(1)} %collective-permute-done.5.refs_8_) | copy-start | bytes 1277956
  102.8 18.3 %collective-permute-start.4 = (bf16[64,3328]{1,0:T(8,128)(2,1)S(1)}, bf16[64,3328]{1,0:T(8,128)(2,1)S(1)}, u32[]{:S(2)}, u32[]{:S(2)}) collective-permute-start(bf16[64,3328]{1,0:T(8,128)(2,1)S(1)} %slice.27), channel_id=1, source_target_pairs={{0,32},{16,48},{32,64},{48,80},{64,96},{80,112},{96,0},{112,16},{1... | collective-permute-start | bytes 1277960 | tf_op jit(solution)/shard_map/ppermute | solution.py:439
  112.0 22.1 %collective-permute-start.7 = (bf16[64,3328]{1,0:T(8,128)(2,1)S(1)}, bf16[64,3328]{1,0:T(8,128)(2,1)S(1)}, u32[]{:S(2)}, u32[]{:S(2)}) collective-permute-start(bf16[64,3328]{1,0:T(8,128)(2,1)S(1)} %collective-permute-done.5.refs_8_), channel_id=1, source_target_pairs={{0,96},{16,112},{32,0},{48,16},{64,32},{80,48},{96,64},{112,80},{1... | collective-permute-start | bytes 1277960 | tf_op jit(solution)/shard_map/ppermute | solution.py:439
  121.1 14.9 %copy-start.7 = (bf16[64,3328]{1,0:T(8,128)(2,1)}, bf16[64,3328]{1,0:T(8,128)(2,1)S(1)}, u32[]{:S(2)}) copy-start(bf16[64,3328]{1,0:T(8,128)(2,1)S(1)} %collective-permute-done.4.refs_7_) | copy-start | bytes 1277956
  121.1 41.6 %collective-permute-start.9 = (bf16[128,3328]{1,0:T(8,128)(2,1)}, bf16[128,3328]{1,0:T(8,128)(2,1)}, u32[]{:S(2)}, u32[]{:S(2)}) collective-permute-start(bf16[128,3328]{1,0:T(8,128)(2,1)} %bitcast.9.refs_2_), channel_id=1, source_target_pairs={{0,32},{16,48},{32,64},{48,80},{64,96},{80,112},{96,0},{112,16},{1... | collective-permute-start | bytes 2555912 | tf_op jit(solution)/shard_map/ppermute | solution.py:439
  121.2 27.1 %collective-permute-start.8 = (bf16[64,3328]{1,0:T(8,128)(2,1)}, bf16[64,3328]{1,0:T(8,128)(2,1)}, u32[]{:S(2)}, u32[]{:S(2)}) collective-permute-start(bf16[64,3328]{1,0:T(8,128)(2,1)} %slice.30), channel_id=1, source_target_pairs={{0,16},{16,0},{32,48},{48,32},{64,80},{80,64},{96,112},{112,96},{1... | collective-permute-start | bytes 1277960 | tf_op jit(solution)/shard_map/ppermute | solution.py:445
  131.8 30.8 %collective-permute-start.13 = (bf16[128,3328]{1,0:T(8,128)(2,1)}, bf16[128,3328]{1,0:T(8,128)(2,1)}, u32[]{:S(2)}, u32[]{:S(2)}) collective-permute-start(bf16[128,3328]{1,0:T(8,128)(2,1)} %collective-permute-done.12.refs_6_), channel_id=1, source_target_pairs={{0,32},{16,48},{32,64},{48,80},{64,96},{80,112},{96,0},{112,16},{1... | collective-permute-start | bytes 2555912 | tf_op jit(solution)/shard_map/ppermute | solution.py:439
  134.1 14.1 %copy-start.4 = (bf16[64,3328]{1,0:T(8,128)(2,1)}, bf16[64,3328]{1,0:T(8,128)(2,1)S(1)}, u32[]{:S(2)}) copy-start(bf16[64,3328]{1,0:T(8,128)(2,1)S(1)} %collective-permute-done.7.low_ref) | copy-start | bytes 1277956
  134.1 28.6 %collective-permute-start.14 = (bf16[128,3328]{1,0:T(8,128)(2,1)}, bf16[128,3328]{1,0:T(8,128)(2,1)}, u32[]{:S(2)}, u32[]{:S(2)}) collective-permute-start(bf16[128,3328]{1,0:T(8,128)(2,1)} %collective-permute-done.12.refs_6_), channel_id=1, source_target_pairs={{0,96},{16,112},{32,0},{48,16},{64,32},{80,48},{96,64},{112,80},{1... | collective-permute-start | bytes 2555912 | tf_op jit(solution)/shard_map/ppermute | solution.py:439
  134.5 36.6 %collective-permute-start.11 = (bf16[128,3328]{1,0:T(8,128)(2,1)}, bf16[128,3328]{1,0:T(8,128)(2,1)}, u32[]{:S(2)}, u32[]{:S(2)}) collective-permute-start(bf16[128,3328]{1,0:T(8,128)(2,1)} %collective-permute-done.10.refs_4_), channel_id=1, source_target_pairs={{0,96},{16,112},{32,0},{48,16},{64,32},{80,48},{96,64},{112,80},{1... | collective-permute-start | bytes 2555912 | tf_op jit(solution)/shard_map/ppermute | solution.py:439
  152.9 45.4 %all-to-all-start.2 = ((bf16[16,64,1024]{2,1,0:T(8,128)(2,1)}), bf16[16,64,1024]{2,1,0:T(8,128)(2,1)}, u32[]{:S(2)}, u32[]{:S(2)}) async-start(bf16[16,64,1024]{2,1,0:T(8,128)(2,1)} %bitcast.22), calls=%async_computation.2 | async-start | bytes 4194304 | tf_op jit(solution)/shard_map/all_to_all | solution.py:449
  162.6 22.0 %collective-permute-start.15 = (bf16[128,3328]{1,0:T(8,128)(2,1)}, bf16[128,3328]{1,0:T(8,128)(2,1)}, u32[]{:S(2)}, u32[]{:S(2)}) collective-permute-start(bf16[128,3328]{1,0:T(8,128)(2,1)} %collective-permute-done.13.refs_7_), channel_id=1, source_target_pairs={{0,32},{16,48},{32,64},{48,80},{64,96},{80,112},{96,0},{112,16},{1... | collective-permute-start | bytes 2555912 | tf_op jit(solution)/shard_map/ppermute | solution.py:439
  189.3 4.3 %collective-permute-start.16 = (bf16[8,64,1024]{2,1,0:T(8,128)(2,1)}, bf16[8,64,1024]{2,1,0:T(8,128)(2,1)S(1)}, u32[]{:S(2)}, u32[]{:S(2)}) collective-permute-start(bf16[8,64,1024]{2,1,0:T(8,128)(2,1)} %get-tuple-element.22), channel_id=1, source_target_pairs={{0,1},{1,0},{2,3},{3,2},{4,5},{5,4},{6,7},{7,6},{8,9},{9,8},{10,11... | collective-permute-start | bytes 3145736 | tf_op jit(solution)/shard_map/ppermute | solution.py:421
  193.6 1.0 copy-start.2
  198.3 19.3 %all-to-all-start.5 = ((bf16[8,64,1024]{2,1,0:T(8,128)(2,1)}), bf16[8,64,1024]{2,1,0:T(8,128)(2,1)S(1)}, u32[]{:S(2)}, u32[]{:S(2)}) async-start(bf16[8,64,1024]{2,1,0:T(8,128)(2,1)} %shard_map.62), calls=%async_computation.5 | async-start | bytes 2097152 | tf_op jit(solution)/shard_map/all_to_all | solution.py:432

commit v4 on v3

--- a/solution.py
+++ b/solution.py
@@ -412,22 +412,10 @@
     )(place, weight, kept, sent, arrived_rows, arrived_rows)
 
 
-def total_kernel(keep_ref, got_ref, out_ref):
-    out_ref[...] = (keep_ref[...] + got_ref[...].astype(jnp.float32)).astype(jnp.bfloat16)
-
-
 def reduce_shares(keep, send):
     count = lax.axis_size("tp")
     got = lax.ppermute(send, "tp", [(i, i ^ 1) for i in range(count)])
-    blocks, rows, columns = keep.shape
-    spec = pl.BlockSpec((blocks // 4, rows, columns), lambda i: (i, 0, 0))
-    total = pl.pallas_call(
-        total_kernel,
-        grid=(4,),
-        out_shape=jax.ShapeDtypeStruct(keep.shape, jnp.bfloat16),
-        in_specs=[spec, spec],
-        out_specs=spec,
-    )(keep, got)
+    total = (keep + got.astype(jnp.float32)).astype(jnp.bfloat16)
     groups = [list(range(core, count, 2)) for core in range(2)]
     parts = lax.all_to_all(total, "tp", 0, 0, axis_index_groups=groups, tiled=True)
     return jnp.sum(parts.astype(jnp.float32), axis=0)

time: 220 us -> 218 us (level)
  Pallas kernels: 64 us -> 60.2 us
  other arithmetic: 7.15 us -> 10.2 us
    pallas_call x1 -> x0, Pallas kernels: 3.76 us -> none  [reduce_shares(): pl.pallas_call(total_kernel, grid=(4,), out_shape=jax.ShapeDtypeStruct(ke...]
    convert_element_type x0 -> x1, other arithmetic: none -> 2.95 us  [reduce_shares(): total = (keep + got.astype(jnp.float32)).astype(jnp.bfloat16)]
  transfers between devices with their start and end apart: 22 -> 22, of which waited for: 10 -> 10; matrix products, arithmetic and copies ran while one was open for 3% -> 4% of each run, Pallas kernels for 26% -> 25%
where the time goes in v4:
time: 218 us; the launch traced here: 217 us
  waiting for transfers between devices  69.5 us (32%)
  Pallas kernels  60.2 us (28%)
  starting transfers between devices  52 us (24%)
  blocking collectives  19 us (9%)
  other arithmetic  10.2 us (5%)
  local copies, waits for them, and re-layouts  5.79 us (3%)
    all_to_all x4, starting transfers between devices, exchange(): return lax.all_to_all(block, 'tp', 0, 0, tiled=True)  27.5 us
    ppermute x12, waiting for transfers between devices, move(): lax.ppermute(block, 'ctx', [(i, (i + 2 * step) % count) for i in range(co...  25.8 us
    all_to_all x1, blocking collectives, exchange(): return lax.all_to_all(block, 'tp', 0, 0, tiled=True)  19 us
    ppermute x4, waiting for transfers between devices, across(): lax.ppermute(block, 'ctx', [(i, i ^ 1) for i in range(lax.axis_size('ctx'...  15.2 us
    pallas_call x1, Pallas kernels, decode_weights(): pl.pallas_call(decode_kernel, grid=(rows // step,), out_shape=jax.ShapeDt...  14.3 us
    all_to_all x4, waiting for transfers between devices, exchange(): return lax.all_to_all(block, 'tp', 0, 0, tiled=True)  13.1 us
    all_to_all x1, waiting for transfers between devices, reduce_shares(): lax.all_to_all(total, 'tp', 0, 0, axis_index_groups=groups, tiled=True)  12.9 us
    ppermute x12, starting transfers between devices, move(): lax.ppermute(block, 'ctx', [(i, (i + 2 * step) % count) for i in range(co...  12.7 us
  transfers between devices with their start and end apart: 22, of which 10 were waited for; matrix products, arithmetic and copies ran while one was open for 4% of the time, Pallas kernels for 25%

profile of v4, /device:TPU:1, one launch (start us, length us, event | category | flops | bytes accessed | tf_op | source)
XLA Modules:
  0.0 216.8 jit_solution(2825429447245596380)
XLA Ops:
  0.7 2.8 %fusion = (bf16[16,8,3328]{2,1,0:T(8,128)(2,1)}, bf16[16,8,3328]{2,1,0:T(8,128)(2,1)}) fusion(bf16[16,2,8,3328]{3,2,1,0:T(8,128)(2,1)} %bitcast.23, bf16[3328]{0:T(1024)(128)(2,1)S(1)} %subtract_convert_fusion), kind=kLoop, calls=%fused_computation.4 | loop fusion | flops 851968 | bytes 3414528 | tf_op jit(solution)/shard_map/mul | solution.py:460
  3.5 7.8 %all-to-all-start = ((bf16[16,8,3328]{2,1,0:T(8,128)(2,1)}), bf16[16,8,3328]{2,1,0:T(8,128)(2,1)S(1)}, u32[]{:S(2)}, u32[]{:S(2)}) async-start(bf16[16,8,3328]{2,1,0:T(8,128)(2,1)} %get-tuple-element.24), calls=%async_computation | async-start | bytes 1703936 | tf_op jit(solution)/shard_map/all_to_all | solution.py:437
  11.3 14.3 %shard_map.55.refs_1_.weight_ref = bf16[3328,1024]{1,0:T(8,128)(2,1)} custom-call(s32[3328,1024]{1,0:T(8,128)} %codes_ref.1, s32[104,1024]{1,0:T(8,128)} %exps_ref.1), custom_call_target="tpu_custom_call" | custom-call | flops 34078720 | bytes 20447232 | tf_op jit(solution)/shard_map/pallas_call | solution.py:69
  26.6 6.1 %shard_map.56 = bf16[16,8,3328]{2,1,0:T(8,128)(2,1)} custom-call(bf16[16,8,3328]{2,1,0:T(8,128)(2,1)} %copy-done.1, bf16[1664,1664]{1,0:T(8,128)(2,1)} %constant.43.clone.refs_1_), custom_call_target="tpu_custom_call" | custom-call | flops 1417674752 | bytes 7241728 | tf_op jit(solution)/shard_map/pallas_call | solution.py:137
  32.7 19.0 %all_to_all.30 = bf16[16,8,3328]{2,1,0:T(8,128)(2,1)S(1)} all-to-all(bf16[16,8,3328]{2,1,0:T(8,128)(2,1)} %shard_map.56), channel_id=1, replica_groups=mesh['ctx'=8,'tp'=16] {'tp'}, dimensions={0} | all-to-all | bytes 1703936 | tf_op jit(solution)/shard_map/all_to_all | solution.py:437
  51.8 4.6 %all-to-all-start.3 = ((bf16[16,8,3328]{2,1,0:T(8,128)(2,1)}), bf16[16,8,3328]{2,1,0:T(8,128)(2,1)S(1)}, u32[]{:S(2)}, u32[]{:S(2)}) async-start(bf16[16,8,3328]{2,1,0:T(8,128)(2,1)} %get-tuple-element.18), calls=%async_computation.3 | async-start | bytes 1703936 | tf_op jit(solution)/shard_map/all_to_all | solution.py:437
  56.3 2.5 %collective-permute-start.3 = (bf16[128,3328]{1,0:T(8,128)(2,1)S(1)}, bf16[128,3328]{1,0:T(8,128)(2,1)S(1)}, u32[]{:S(2)}, u32[]{:S(2)}) collective-permute-start(bf16[128,3328]{1,0:T(8,128)(2,1)S(1)} %bitcast.26), channel_id=1, source_target_pairs={{0,16},{16,0},{32,48},{48,32},{64,80},{80,64},{96,112},{112,96},{1... | collective-permute-start | bytes 2555912 | tf_op jit(solution)/shard_map/ppermute | solution.py:433
  61.5 8.6 %all-to-all-done.3.refs_0_ = bf16[16,8,3328]{2,1,0:T(8,128)(2,1)S(1)} async-done(((bf16[16,8,3328]{2,1,0:T(8,128)(2,1)}), bf16[16,8,3328]{2,1,0:T(8,128)(2,1)S(1)}, u32[]{:S(2)}, u32[]{:S(2)}) %all-to-all-start.3) | async-done | bytes 852000 | tf_op jit(solution)/shard_map/all_to_all | solution.py:437
  71.0 6.1 %shard_map.59 = bf16[16,8,3328]{2,1,0:T(8,128)(2,1)} custom-call(bf16[16,8,3328]{2,1,0:T(8,128)(2,1)} %copy-done, bf16[1664,1664]{1,0:T(8,128)(2,1)} %constant.43.clone.refs_1_), custom_call_target="tpu_custom_call" | custom-call | flops 1417674752 | bytes 7241728 | tf_op jit(solution)/shard_map/pallas_call | solution.py:137
  77.1 5.4 %all-to-all-start.4 = ((bf16[16,8,3328]{2,1,0:T(8,128)(2,1)}), bf16[16,8,3328]{2,1,0:T(8,128)(2,1)}, u32[]{:S(2)}, u32[]{:S(2)}) async-start(bf16[16,8,3328]{2,1,0:T(8,128)(2,1)} %shard_map.59), calls=%async_computation.4 | async-start | bytes 1703936 | tf_op jit(solution)/shard_map/all_to_all | solution.py:437
  82.5 5.0 %collective-permute-done.3.refs_6_ = bf16[128,3328]{1,0:T(8,128)(2,1)S(1)} collective-permute-done((bf16[128,3328]{1,0:T(8,128)(2,1)S(1)}, bf16[128,3328]{1,0:T(8,128)(2,1)S(1)}, u32[]{:S(2)}, u32[]{:S(2)}) %collective-permute-start.3) | collective-permute-done | bytes 852000 | tf_op jit(solution)/shard_map/ppermute | solution.py:433
  87.5 2.8 %collective-permute-start.5 = (bf16[64,3328]{1,0:T(8,128)(2,1)S(1)}, bf16[64,3328]{1,0:T(8,128)(2,1)S(1)}, u32[]{:S(2)}, u32[]{:S(2)}) collective-permute-start(bf16[64,3328]{1,0:T(8,128)(2,1)S(1)} %slice.27), channel_id=1, source_target_pairs={{0,96},{16,112},{32,0},{48,16},{64,32},{80,48},{96,64},{112,80},{1... | collective-permute-start | bytes 1277960 | tf_op jit(solution)/shard_map/ppermute | solution.py:427
  93.1 4.6 %all-to-all-done.4 = bf16[16,8,3328]{2,1,0:T(8,128)(2,1)} async-done(((bf16[16,8,3328]{2,1,0:T(8,128)(2,1)}), bf16[16,8,3328]{2,1,0:T(8,128)(2,1)}, u32[]{:S(2)}, u32[]{:S(2)}) %all-to-all-start.4) | async-done | bytes 852000 | tf_op jit(solution)/shard_map/all_to_all | solution.py:437
  97.6 2.4 %collective-permute-start.12 = (bf16[128,3328]{1,0:T(8,128)(2,1)}, bf16[128,3328]{1,0:T(8,128)(2,1)}, u32[]{:S(2)}, u32[]{:S(2)}) collective-permute-start(bf16[128,3328]{1,0:T(8,128)(2,1)} %bitcast.9.refs_2_), channel_id=1, source_target_pairs={{0,16},{16,0},{32,48},{48,32},{64,80},{80,64},{96,112},{112,96},{1... | collective-permute-start | bytes 2555912 | tf_op jit(solution)/shard_map/ppermute | solution.py:433
  100.1 2.7 %collective-permute-start.10 = (bf16[128,3328]{1,0:T(8,128)(2,1)}, bf16[128,3328]{1,0:T(8,128)(2,1)}, u32[]{:S(2)}, u32[]{:S(2)}) collective-permute-start(bf16[128,3328]{1,0:T(8,128)(2,1)} %bitcast.9.refs_2_), channel_id=1, source_target_pairs={{0,96},{16,112},{32,0},{48,16},{64,32},{80,48},{96,64},{112,80},{1... | collective-permute-start | bytes 2555912 | tf_op jit(solution)/shard_map/ppermute | solution.py:427
  102.8 9.4 %collective-permute-done.2.refs_5_ = bf16[128,3328]{1,0:T(8,128)(2,1)} collective-permute-done((bf16[128,3328]{1,0:T(8,128)(2,1)}, bf16[128,3328]{1,0:T(8,128)(2,1)}, u32[]{:S(2)}, u32[]{:S(2)}) %collective-permute-start.2) | collective-permute-done | bytes 852000 | tf_op jit(solution)/shard_map/ppermute | solution.py:427
  112.8 1.8 slice.30
  114.6 6.7 %collective-permute-done.4.refs_7_ = bf16[64,3328]{1,0:T(8,128)(2,1)S(1)} collective-permute-done((bf16[64,3328]{1,0:T(8,128)(2,1)S(1)}, bf16[64,3328]{1,0:T(8,128)(2,1)S(1)}, u32[]{:S(2)}, u32[]{:S(2)}) %collective-permute-start.4) | collective-permute-done | bytes 426016 | tf_op jit(solution)/shard_map/ppermute | solution.py:427
  121.7 10.1 %collective-permute-done.12.refs_6_ = bf16[128,3328]{1,0:T(8,128)(2,1)} collective-permute-done((bf16[128,3328]{1,0:T(8,128)(2,1)}, bf16[128,3328]{1,0:T(8,128)(2,1)}, u32[]{:S(2)}, u32[]{:S(2)}) %collective-permute-start.12) | collective-permute-done | bytes 852000 | tf_op jit(solution)/shard_map/ppermute | solution.py:433
  131.8 2.3 %collective-permute-start.13 = (bf16[128,3328]{1,0:T(8,128)(2,1)}, bf16[128,3328]{1,0:T(8,128)(2,1)}, u32[]{:S(2)}, u32[]{:S(2)}) collective-permute-start(bf16[128,3328]{1,0:T(8,128)(2,1)} %collective-permute-done.12.refs_6_), channel_id=1, source_target_pairs={{0,32},{16,48},{32,64},{48,80},{64,96},{80,112},{96,0},{112,16},{1... | collective-permute-start | bytes 2555912 | tf_op jit(solution)/shard_map/ppermute | solution.py:427
  136.1 12.1 %shard_map.57.before_ref = bf16[8,128,1024]{2,1,0:T(8,128)(2,1)} custom-call(s32[3]{0:T(128)} %pad_add_fusion.refs_0_.place_ref, bf16[3328,1024]{1,0:T(8,128)(2,1)} %shard_map.55.refs_1_.weight_ref, bf16[128,3328]{1,0:T(8,128)(2,1)} %bitcast.29, bf16[128,3328]{1,0:T(8,128)(2,1)} %collective-permute-done.refs_3_, ...), custom_call_target="tpu_custom_call" | custom-call | flops 152672665600 | bytes 14614528 | tf_op jit(solution)/shard_map/pallas_call | solution.py:199
  148.3 4.6 %shard_map.58 = bf16[8,128,1024]{2,1,0:T(8,128)(2,1)} custom-call(s32[3]{0:T(128)} %pad_add_fusion.refs_0_.place_ref, bf16[3328,1024]{1,0:T(8,128)(2,1)} %shard_map.55.refs_1_.weight_ref, bf16[8,128,1024]{2,1,0:T(8,128)(2,1)} %shard_map.57.before_ref, bf16[64,3328]{1,0:T(8,128)(2,1)} %copy-done.3, ...), custom_call_target="tpu_custom_call", output_to_operand_aliasing={{}: (2, {})} | custom-call | flops 872415232 | bytes 7929856 | tf_op jit(solution)/shard_map/pallas_call | solution.py:252
  152.9 9.7 %all-to-all-start.2 = ((bf16[16,64,1024]{2,1,0:T(8,128)(2,1)}), bf16[16,64,1024]{2,1,0:T(8,128)(2,1)}, u32[]{:S(2)}, u32[]{:S(2)}) async-start(bf16[16,64,1024]{2,1,0:T(8,128)(2,1)} %bitcast.22), calls=%async_computation.2 | async-start | bytes 4194304 | tf_op jit(solution)/shard_map/all_to_all | solution.py:437
  162.7 8.3 %collective-permute-done.11.refs_5_ = bf16[128,3328]{1,0:T(8,128)(2,1)} collective-permute-done((bf16[128,3328]{1,0:T(8,128)(2,1)}, bf16[128,3328]{1,0:T(8,128)(2,1)}, u32[]{:S(2)}, u32[]{:S(2)}) %collective-permute-start.11) | collective-permute-done | bytes 852000 | tf_op jit(solution)/shard_map/ppermute | solution.py:427
  171.0 12.3 %shard_map.60 = (f32[8,64,1024]{2,1,0:T(8,128)}, bf16[8,64,1024]{2,1,0:T(8,128)(2,1)}) custom-call(s32[3]{0:T(128)} %pad_add_fusion.refs_0_.place_ref, bf16[3328,1024]{1,0:T(8,128)(2,1)} %shard_map.55.refs_1_.weight_ref, bf16[128,3328]{1,0:T(8,128)(2,1)} %bitcast.9.refs_2_, bf16[128,3328]{1,0:T(8,128)(2,1)} %collective-permute-done.9.refs_3_, ...), custom_call_target="tpu_custom_call" | custom-call | flops 152672665600 | bytes 14614528 | tf_op jit(solution)/shard_map/pallas_call | solution.py:317
  184.6 4.7 %shard_map.61 = (f32[8,64,1024]{2,1,0:T(8,128)}, bf16[8,64,1024]{2,1,0:T(8,128)(2,1)}) custom-call(s32[3]{0:T(128)} %pad_add_fusion.refs_0_.place_ref, bf16[3328,1024]{1,0:T(8,128)(2,1)} %shard_map.55.refs_1_.weight_ref, f32[8,64,1024]{2,1,0:T(8,128)} %get-tuple-element.19.kept, ...), custom_call_target="tpu_custom_call", output_to_operand_aliasing={{0}: (2, {}), {1}: (3, {})} | custom-call | flops 872415232 | bytes 7929856 | tf_op jit(solution)/shard_map/pallas_call | solution.py:383
  189.3 1.8 collective-permute-start.16
  191.1 2.5 %collective-permute-done.16 = bf16[8,64,1024]{2,1,0:T(8,128)(2,1)S(1)} collective-permute-done((bf16[8,64,1024]{2,1,0:T(8,128)(2,1)}, bf16[8,64,1024]{2,1,0:T(8,128)(2,1)S(1)}, u32[]{:S(2)}, u32[]{:S(2)}) %collective-permute-start.16) | collective-permute-done | bytes 1048608 | tf_op jit(solution)/shard_map/ppermute | solution.py:417
  193.6 3.0 %add_convert_fusion = bf16[8,64,1024]{2,1,0:T(8,128)(2,1)} fusion(f32[8,64,1024]{2,1,0:T(8,128)} %get-tuple-element.21, bf16[8,64,1024]{2,1,0:T(8,128)(2,1)S(1)} %collective-permute-done.16), kind=kLoop, calls=%fused_computation.2 | loop fusion | flops 1572864 | bytes 4194304 | tf_op jit(solution)/shard_map/convert_element_type | solution.py:418
  196.6 4.3 %all-to-all-start.5 = ((bf16[8,64,1024]{2,1,0:T(8,128)(2,1)}), bf16[8,64,1024]{2,1,0:T(8,128)(2,1)S(1)}, u32[]{:S(2)}, u32[]{:S(2)}) async-start(bf16[8,64,1024]{2,1,0:T(8,128)(2,1)} %add_convert_fusion), calls=%async_computation.5 | async-start | bytes 2097152 | tf_op jit(solution)/shard_map/all_to_all | solution.py:420
  200.9 2.0 convert_reduce_fusion
  202.9 12.9 %all-to-all-done.5 = bf16[8,64,1024]{2,1,0:T(8,128)(2,1)S(1)} async-done(((bf16[8,64,1024]{2,1,0:T(8,128)(2,1)}), bf16[8,64,1024]{2,1,0:T(8,128)(2,1)S(1)}, u32[]{:S(2)}, u32[]{:S(2)}) %all-to-all-start.5) | async-done | bytes 1048608 | tf_op jit(solution)/shard_map/all_to_all | solution.py:420
  (46 shorter events, 13.4 us)
Async XLA Ops:
  3.5 22.0 %all-to-all-start = ((bf16[16,8,3328]{2,1,0:T(8,128)(2,1)}), bf16[16,8,3328]{2,1,0:T(8,128)(2,1)S(1)}, u32[]{:S(2)}, u32[]{:S(2)}) async-start(bf16[16,8,3328]{2,1,0:T(8,128)(2,1)} %get-tuple-element.24), calls=%async_computation | async-start | bytes 1703936 | tf_op jit(solution)/shard_map/all_to_all | solution.py:437
  25.6 1.0 copy-start.1
  51.7 25.3 %copy-start.2 = (bf16[16,8,3328]{2,1,0:T(8,128)(2,1)}, bf16[16,8,3328]{2,1,0:T(8,128)(2,1)S(1)}, u32[]{:S(2)}) copy-start(bf16[16,8,3328]{2,1,0:T(8,128)(2,1)S(1)} %all_to_all.30) | copy-start | bytes 2555908
  51.8 18.3 %all-to-all-start.3 = ((bf16[16,8,3328]{2,1,0:T(8,128)(2,1)}), bf16[16,8,3328]{2,1,0:T(8,128)(2,1)S(1)}, u32[]{:S(2)}, u32[]{:S(2)}) async-start(bf16[16,8,3328]{2,1,0:T(8,128)(2,1)} %get-tuple-element.18), calls=%async_computation.3 | async-start | bytes 1703936 | tf_op jit(solution)/shard_map/all_to_all | solution.py:437
  56.3 31.2 %collective-permute-start.3 = (bf16[128,3328]{1,0:T(8,128)(2,1)S(1)}, bf16[128,3328]{1,0:T(8,128)(2,1)S(1)}, u32[]{:S(2)}, u32[]{:S(2)}) collective-permute-start(bf16[128,3328]{1,0:T(8,128)(2,1)S(1)} %bitcast.26), channel_id=1, source_target_pairs={{0,16},{16,0},{32,48},{48,32},{64,80},{80,64},{96,112},{112,96},{1... | collective-permute-start | bytes 2555912 | tf_op jit(solution)/shard_map/ppermute | solution.py:433
  58.8 31.6 %collective-permute-start = (bf16[128,3328]{1,0:T(8,128)(2,1)S(1)}, bf16[128,3328]{1,0:T(8,128)(2,1)}, u32[]{:S(2)}, u32[]{:S(2)}) collective-permute-start(bf16[128,3328]{1,0:T(8,128)(2,1)S(1)} %bitcast.27), channel_id=1, source_target_pairs={{0,32},{16,48},{32,64},{48,80},{64,96},{80,112},{96,0},{112,16},{1... | collective-permute-start | bytes 2555912 | tf_op jit(solution)/shard_map/ppermute | solution.py:427
  60.1 31.4 %collective-permute-start.1 = (bf16[128,3328]{1,0:T(8,128)(2,1)S(1)}, bf16[128,3328]{1,0:T(8,128)(2,1)}, u32[]{:S(2)}, u32[]{:S(2)}) collective-permute-start(bf16[128,3328]{1,0:T(8,128)(2,1)S(1)} %bitcast.28), channel_id=1, source_target_pairs={{0,96},{16,112},{32,0},{48,16},{64,32},{80,48},{96,64},{112,80},{1... | collective-permute-start | bytes 2555912 | tf_op jit(solution)/shard_map/ppermute | solution.py:427
  70.1 0.9 copy-start
  77.1 20.5 %all-to-all-start.4 = ((bf16[16,8,3328]{2,1,0:T(8,128)(2,1)}), bf16[16,8,3328]{2,1,0:T(8,128)(2,1)}, u32[]{:S(2)}, u32[]{:S(2)}) async-start(bf16[16,8,3328]{2,1,0:T(8,128)(2,1)} %shard_map.59), calls=%async_computation.4 | async-start | bytes 1703936 | tf_op jit(solution)/shard_map/all_to_all | solution.py:437
  87.5 5.1 %copy-start.4 = (bf16[128,3328]{1,0:T(8,128)(2,1)}, bf16[128,3328]{1,0:T(8,128)(2,1)S(1)}, u32[]{:S(2)}) copy-start(bf16[128,3328]{1,0:T(8,128)(2,1)S(1)} %collective-permute-done.3.refs_6_) | copy-start | bytes 2555908
  87.5 15.3 %collective-permute-start.5 = (bf16[64,3328]{1,0:T(8,128)(2,1)S(1)}, bf16[64,3328]{1,0:T(8,128)(2,1)S(1)}, u32[]{:S(2)}, u32[]{:S(2)}) collective-permute-start(bf16[64,3328]{1,0:T(8,128)(2,1)S(1)} %slice.27), channel_id=1, source_target_pairs={{0,96},{16,112},{32,0},{48,16},{64,32},{80,48},{96,64},{112,80},{1... | collective-permute-start | bytes 1277960 | tf_op jit(solution)/shard_map/ppermute | solution.py:427
  91.4 20.9 %collective-permute-start.2 = (bf16[128,3328]{1,0:T(8,128)(2,1)}, bf16[128,3328]{1,0:T(8,128)(2,1)}, u32[]{:S(2)}, u32[]{:S(2)}) collective-permute-start(bf16[128,3328]{1,0:T(8,128)(2,1)} %collective-permute-done.refs_3_), channel_id=1, source_target_pairs={{0,32},{16,48},{32,64},{48,80},{64,96},{80,112},{96,0},{112,16},{1... | collective-permute-start | bytes 2555912 | tf_op jit(solution)/shard_map/ppermute | solution.py:427
  92.6 28.8 %collective-permute-start.6 = (bf16[128,3328]{1,0:T(8,128)(2,1)S(1)}, bf16[128,3328]{1,0:T(8,128)(2,1)}, u32[]{:S(2)}, u32[]{:S(2)}) collective-permute-start(bf16[128,3328]{1,0:T(8,128)(2,1)S(1)} %pad_maximum_fusion), channel_id=1, source_target_pairs={{0,16},{16,0},{32,48},{48,32},{64,80},{80,64},{96,112},{112,96},{1... | collective-permute-start | bytes 2555912 | tf_op jit(solution)/shard_map/ppermute | solution.py:433
  97.6 34.2 %collective-permute-start.12 = (bf16[128,3328]{1,0:T(8,128)(2,1)}, bf16[128,3328]{1,0:T(8,128)(2,1)}, u32[]{:S(2)}, u32[]{:S(2)}) collective-permute-start(bf16[128,3328]{1,0:T(8,128)(2,1)} %bitcast.9.refs_2_), channel_id=1, source_target_pairs={{0,16},{16,0},{32,48},{48,32},{64,80},{80,64},{96,112},{112,96},{1... | collective-permute-start | bytes 2555912 | tf_op jit(solution)/shard_map/ppermute | solution.py:433
  100.1 34.4 %collective-permute-start.10 = (bf16[128,3328]{1,0:T(8,128)(2,1)}, bf16[128,3328]{1,0:T(8,128)(2,1)}, u32[]{:S(2)}, u32[]{:S(2)}) collective-permute-start(bf16[128,3328]{1,0:T(8,128)(2,1)} %bitcast.9.refs_2_), channel_id=1, source_target_pairs={{0,96},{16,112},{32,0},{48,16},{64,32},{80,48},{96,64},{112,80},{1... | collective-permute-start | bytes 2555912 | tf_op jit(solution)/shard_map/ppermute | solution.py:427
  102.8 33.3 %copy-start.5 = (bf16[64,3328]{1,0:T(8,128)(2,1)}, bf16[64,3328]{1,0:T(8,128)(2,1)S(1)}, u32[]{:S(2)}) copy-start(bf16[64,3328]{1,0:T(8,128)(2,1)S(1)} %collective-permute-done.5.refs_8_) | copy-start | bytes 1277956
  102.8 18.5 %collective-permute-start.4 = (bf16[64,3328]{1,0:T(8,128)(2,1)S(1)}, bf16[64,3328]{1,0:T(8,128)(2,1)S(1)}, u32[]{:S(2)}, u32[]{:S(2)}) collective-permute-start(bf16[64,3328]{1,0:T(8,128)(2,1)S(1)} %slice.27), channel_id=1, source_target_pairs={{0,32},{16,48},{32,64},{48,80},{64,96},{80,112},{96,0},{112,16},{1... | collective-permute-start | bytes 1277960 | tf_op jit(solution)/shard_map/ppermute | solution.py:427
  112.2 21.9 %collective-permute-start.7 = (bf16[64,3328]{1,0:T(8,128)(2,1)S(1)}, bf16[64,3328]{1,0:T(8,128)(2,1)S(1)}, u32[]{:S(2)}, u32[]{:S(2)}) collective-permute-start(bf16[64,3328]{1,0:T(8,128)(2,1)S(1)} %collective-permute-done.5.refs_8_), channel_id=1, source_target_pairs={{0,96},{16,112},{32,0},{48,16},{64,32},{80,48},{96,64},{112,80},{1... | collective-permute-start | bytes 1277960 | tf_op jit(solution)/shard_map/ppermute | solution.py:427
  121.4 14.7 %copy-start.6 = (bf16[64,3328]{1,0:T(8,128)(2,1)}, bf16[64,3328]{1,0:T(8,128)(2,1)S(1)}, u32[]{:S(2)}) copy-start(bf16[64,3328]{1,0:T(8,128)(2,1)S(1)} %collective-permute-done.4.refs_7_) | copy-start | bytes 1277956
  121.4 41.3 %collective-permute-start.9 = (bf16[128,3328]{1,0:T(8,128)(2,1)}, bf16[128,3328]{1,0:T(8,128)(2,1)}, u32[]{:S(2)}, u32[]{:S(2)}) collective-permute-start(bf16[128,3328]{1,0:T(8,128)(2,1)} %bitcast.9.refs_2_), channel_id=1, source_target_pairs={{0,32},{16,48},{32,64},{48,80},{64,96},{80,112},{96,0},{112,16},{1... | collective-permute-start | bytes 2555912 | tf_op jit(solution)/shard_map/ppermute | solution.py:427
  121.4 26.9 %collective-permute-start.8 = (bf16[64,3328]{1,0:T(8,128)(2,1)}, bf16[64,3328]{1,0:T(8,128)(2,1)}, u32[]{:S(2)}, u32[]{:S(2)}) collective-permute-start(bf16[64,3328]{1,0:T(8,128)(2,1)} %slice.30), channel_id=1, source_target_pairs={{0,16},{16,0},{32,48},{48,32},{64,80},{80,64},{96,112},{112,96},{1... | collective-permute-start | bytes 1277960 | tf_op jit(solution)/shard_map/ppermute | solution.py:433
  131.8 30.8 %collective-permute-start.13 = (bf16[128,3328]{1,0:T(8,128)(2,1)}, bf16[128,3328]{1,0:T(8,128)(2,1)}, u32[]{:S(2)}, u32[]{:S(2)}) collective-permute-start(bf16[128,3328]{1,0:T(8,128)(2,1)} %collective-permute-done.12.refs_6_), channel_id=1, source_target_pairs={{0,32},{16,48},{32,64},{48,80},{64,96},{80,112},{96,0},{112,16},{1... | collective-permute-start | bytes 2555912 | tf_op jit(solution)/shard_map/ppermute | solution.py:427
  134.1 14.1 %copy-start.3 = (bf16[64,3328]{1,0:T(8,128)(2,1)}, bf16[64,3328]{1,0:T(8,128)(2,1)S(1)}, u32[]{:S(2)}) copy-start(bf16[64,3328]{1,0:T(8,128)(2,1)S(1)} %collective-permute-done.7.low_ref) | copy-start | bytes 1277956
  134.1 28.6 %collective-permute-start.14 = (bf16[128,3328]{1,0:T(8,128)(2,1)}, bf16[128,3328]{1,0:T(8,128)(2,1)}, u32[]{:S(2)}, u32[]{:S(2)}) collective-permute-start(bf16[128,3328]{1,0:T(8,128)(2,1)} %collective-permute-done.12.refs_6_), channel_id=1, source_target_pairs={{0,96},{16,112},{32,0},{48,16},{64,32},{80,48},{96,64},{112,80},{1... | collective-permute-start | bytes 2555912 | tf_op jit(solution)/shard_map/ppermute | solution.py:427
  134.5 36.6 %collective-permute-start.11 = (bf16[128,3328]{1,0:T(8,128)(2,1)}, bf16[128,3328]{1,0:T(8,128)(2,1)}, u32[]{:S(2)}, u32[]{:S(2)}) collective-permute-start(bf16[128,3328]{1,0:T(8,128)(2,1)} %collective-permute-done.10.refs_4_), channel_id=1, source_target_pairs={{0,96},{16,112},{32,0},{48,16},{64,32},{80,48},{96,64},{112,80},{1... | collective-permute-start | bytes 2555912 | tf_op jit(solution)/shard_map/ppermute | solution.py:427
  152.9 43.7 %all-to-all-start.2 = ((bf16[16,64,1024]{2,1,0:T(8,128)(2,1)}), bf16[16,64,1024]{2,1,0:T(8,128)(2,1)}, u32[]{:S(2)}, u32[]{:S(2)}) async-start(bf16[16,64,1024]{2,1,0:T(8,128)(2,1)} %bitcast.22), calls=%async_computation.2 | async-start | bytes 4194304 | tf_op jit(solution)/shard_map/all_to_all | solution.py:437
  162.6 22.0 %collective-permute-start.15 = (bf16[128,3328]{1,0:T(8,128)(2,1)}, bf16[128,3328]{1,0:T(8,128)(2,1)}, u32[]{:S(2)}, u32[]{:S(2)}) collective-permute-start(bf16[128,3328]{1,0:T(8,128)(2,1)} %collective-permute-done.13.refs_7_), channel_id=1, source_target_pairs={{0,32},{16,48},{32,64},{48,80},{64,96},{80,112},{96,0},{112,16},{1... | collective-permute-start | bytes 2555912 | tf_op jit(solution)/shard_map/ppermute | solution.py:427
  189.3 4.3 %collective-permute-start.16 = (bf16[8,64,1024]{2,1,0:T(8,128)(2,1)}, bf16[8,64,1024]{2,1,0:T(8,128)(2,1)S(1)}, u32[]{:S(2)}, u32[]{:S(2)}) collective-permute-start(bf16[8,64,1024]{2,1,0:T(8,128)(2,1)} %get-tuple-element.22), channel_id=1, source_target_pairs={{0,1},{1,0},{2,3},{3,2},{4,5},{5,4},{6,7},{7,6},{8,9},{9,8},{10,11... | collective-permute-start | bytes 3145736 | tf_op jit(solution)/shard_map/ppermute | solution.py:417
  196.6 19.3 %all-to-all-start.5 = ((bf16[8,64,1024]{2,1,0:T(8,128)(2,1)}), bf16[8,64,1024]{2,1,0:T(8,128)(2,1)S(1)}, u32[]{:S(2)}, u32[]{:S(2)}) async-start(bf16[8,64,1024]{2,1,0:T(8,128)(2,1)} %add_convert_fusion), calls=%async_computation.5 | async-start | bytes 2097152 | tf_op jit(solution)/shard_map/all_to_all | solution.py:420

commit v5 on v4

--- a/solution.py
+++ b/solution.py
@@ -492,10 +492,10 @@
     part0 = product_last(place, weight, part0, last0, late_far0)
     sent0 = exchange(part0.reshape(groups, half, columns))
     other_below1, other_above1 = up(other1), down(other1)
-    far1 = [down(above1)]
+    far1 = [up(below1)]
     other_below1, other_above1, *far1 = keep(other_below1, other_above1, *far1)
 
-    last1 = [up(other_below1)]
+    last1 = [down(other_above1)]
     spec1 = [(index, 0, rows, index, 0) for index in range(7)]
     pieces1 = [own1, below1, above1, *far1, other1, other_below1, other_above1]
     kept, sent = split_product(place, weight, spec1, pieces1)

time: 218 us -> 229 us (1.050)
  waiting for transfers between devices: 69.5 us -> 80 us
    ppermute x12, waiting for transfers between devices: 25.8 us -> 46.4 us  [move(): lax.ppermute(block, 'ctx', [(i, (i + 2 * step) % count) for i in range(co...]
    ppermute x4, waiting for transfers between devices: 15.2 us -> 5.03 us  [across(): lax.ppermute(block, 'ctx', [(i, i ^ 1) for i in range(lax.axis_size('ctx'...]
  transfers between devices with their start and end apart: 22 -> 22, of which waited for: 10 -> 9; matrix products, arithmetic and copies ran while one was open for 4% -> 4% of each run, Pallas kernels for 25% -> 24%
where the time goes in v5:
time: 229 us; the launch traced here: 228 us
  waiting for transfers between devices  80 us (35%)
  Pallas kernels  60.2 us (26%)
  starting transfers between devices  52.5 us (23%)
  blocking collectives  19 us (8%)
  other arithmetic  10.2 us (4%)
  local copies, waits for them, and re-layouts  5.79 us (3%)
    ppermute x12, waiting for transfers between devices, move(): lax.ppermute(block, 'ctx', [(i, (i + 2 * step) % count) for i in range(co...  46.4 us
    all_to_all x4, starting transfers between devices, exchange(): return lax.all_to_all(block, 'tp', 0, 0, tiled=True)  26.6 us
    all_to_all x1, blocking collectives, exchange(): return lax.all_to_all(block, 'tp', 0, 0, tiled=True)  19 us
    pallas_call x1, Pallas kernels, decode_weights(): pl.pallas_call(decode_kernel, grid=(rows // step,), out_shape=jax.ShapeDt...  14.3 us
    all_to_all x4, waiting for transfers between devices, exchange(): return lax.all_to_all(block, 'tp', 0, 0, tiled=True)  13.1 us
    all_to_all x1, waiting for transfers between devices, reduce_shares(): lax.all_to_all(total, 'tp', 0, 0, axis_index_groups=groups, tiled=True)  12.9 us
    ppermute x12, starting transfers between devices, move(): lax.ppermute(block, 'ctx', [(i, (i + 2 * step) % count) for i in range(co...  12.6 us
    pallas_call x1, Pallas kernels, split_product(): pl.pallas_call(lambda *refs: split_product_kernel(spec, shifts, *refs), g...  12.3 us
  transfers between devices with their start and end apart: 22, of which 9 were waited for; matrix products, arithmetic and copies ran while one was open for 4% of the time, Pallas kernels for 24%

profile of v5, /device:TPU:1, one launch (start us, length us, event | category | flops | bytes accessed | tf_op | source)
XLA Modules:
  0.0 227.9 jit_solution(16037035159935368221)
XLA Ops:
  0.7 2.8 %fusion = (bf16[16,8,3328]{2,1,0:T(8,128)(2,1)}, bf16[16,8,3328]{2,1,0:T(8,128)(2,1)}) fusion(bf16[16,2,8,3328]{3,2,1,0:T(8,128)(2,1)} %bitcast.23, bf16[3328]{0:T(1024)(128)(2,1)S(1)} %subtract_convert_fusion), kind=kLoop, calls=%fused_computation.4 | loop fusion | flops 851968 | bytes 3414528 | tf_op jit(solution)/shard_map/mul | solution.py:460
  3.5 7.8 %all-to-all-start = ((bf16[16,8,3328]{2,1,0:T(8,128)(2,1)}), bf16[16,8,3328]{2,1,0:T(8,128)(2,1)S(1)}, u32[]{:S(2)}, u32[]{:S(2)}) async-start(bf16[16,8,3328]{2,1,0:T(8,128)(2,1)} %get-tuple-element.24), calls=%async_computation | async-start | bytes 1703936 | tf_op jit(solution)/shard_map/all_to_all | solution.py:437
  11.3 14.3 %shard_map.55.refs_1_.weight_ref = bf16[3328,1024]{1,0:T(8,128)(2,1)} custom-call(s32[3328,1024]{1,0:T(8,128)} %codes_ref.1, s32[104,1024]{1,0:T(8,128)} %exps_ref.1), custom_call_target="tpu_custom_call" | custom-call | flops 34078720 | bytes 20447232 | tf_op jit(solution)/shard_map/pallas_call | solution.py:69
  26.6 6.1 %shard_map.56 = bf16[16,8,3328]{2,1,0:T(8,128)(2,1)} custom-call(bf16[16,8,3328]{2,1,0:T(8,128)(2,1)} %copy-done.1, bf16[1664,1664]{1,0:T(8,128)(2,1)} %constant.43.clone.refs_1_), custom_call_target="tpu_custom_call" | custom-call | flops 1417674752 | bytes 7241728 | tf_op jit(solution)/shard_map/pallas_call | solution.py:137
  32.7 19.0 %all_to_all.30 = bf16[16,8,3328]{2,1,0:T(8,128)(2,1)S(1)} all-to-all(bf16[16,8,3328]{2,1,0:T(8,128)(2,1)} %shard_map.56), channel_id=1, replica_groups=mesh['ctx'=8,'tp'=16] {'tp'}, dimensions={0} | all-to-all | bytes 1703936 | tf_op jit(solution)/shard_map/all_to_all | solution.py:437
  51.8 4.6 %all-to-all-start.3 = ((bf16[16,8,3328]{2,1,0:T(8,128)(2,1)}), bf16[16,8,3328]{2,1,0:T(8,128)(2,1)S(1)}, u32[]{:S(2)}, u32[]{:S(2)}) async-start(bf16[16,8,3328]{2,1,0:T(8,128)(2,1)} %get-tuple-element.18), calls=%async_computation.3 | async-start | bytes 1703936 | tf_op jit(solution)/shard_map/all_to_all | solution.py:437
  56.3 2.5 %collective-permute-start.3 = (bf16[128,3328]{1,0:T(8,128)(2,1)S(1)}, bf16[128,3328]{1,0:T(8,128)(2,1)S(1)}, u32[]{:S(2)}, u32[]{:S(2)}) collective-permute-start(bf16[128,3328]{1,0:T(8,128)(2,1)S(1)} %bitcast.26), channel_id=1, source_target_pairs={{0,16},{16,0},{32,48},{48,32},{64,80},{80,64},{96,112},{112,96},{1... | collective-permute-start | bytes 2555912 | tf_op jit(solution)/shard_map/ppermute | solution.py:433
  61.5 8.6 %all-to-all-done.3.refs_0_ = bf16[16,8,3328]{2,1,0:T(8,128)(2,1)S(1)} async-done(((bf16[16,8,3328]{2,1,0:T(8,128)(2,1)}), bf16[16,8,3328]{2,1,0:T(8,128)(2,1)S(1)}, u32[]{:S(2)}, u32[]{:S(2)}) %all-to-all-start.3) | async-done | bytes 852000 | tf_op jit(solution)/shard_map/all_to_all | solution.py:437
  71.0 6.1 %shard_map.59 = bf16[16,8,3328]{2,1,0:T(8,128)(2,1)} custom-call(bf16[16,8,3328]{2,1,0:T(8,128)(2,1)} %copy-done, bf16[1664,1664]{1,0:T(8,128)(2,1)} %constant.43.clone.refs_1_), custom_call_target="tpu_custom_call" | custom-call | flops 1417674752 | bytes 7241728 | tf_op jit(solution)/shard_map/pallas_call | solution.py:137
  77.1 5.4 %all-to-all-start.4 = ((bf16[16,8,3328]{2,1,0:T(8,128)(2,1)}), bf16[16,8,3328]{2,1,0:T(8,128)(2,1)}, u32[]{:S(2)}, u32[]{:S(2)}) async-start(bf16[16,8,3328]{2,1,0:T(8,128)(2,1)} %shard_map.59), calls=%async_computation.4 | async-start | bytes 1703936 | tf_op jit(solution)/shard_map/all_to_all | solution.py:437
  82.5 5.0 %collective-permute-done.3.refs_6_ = bf16[128,3328]{1,0:T(8,128)(2,1)S(1)} collective-permute-done((bf16[128,3328]{1,0:T(8,128)(2,1)S(1)}, bf16[128,3328]{1,0:T(8,128)(2,1)S(1)}, u32[]{:S(2)}, u32[]{:S(2)}) %collective-permute-start.3) | collective-permute-done | bytes 852000 | tf_op jit(solution)/shard_map/ppermute | solution.py:433
  87.5 2.8 %collective-permute-start.5 = (bf16[64,3328]{1,0:T(8,128)(2,1)S(1)}, bf16[64,3328]{1,0:T(8,128)(2,1)S(1)}, u32[]{:S(2)}, u32[]{:S(2)}) collective-permute-start(bf16[64,3328]{1,0:T(8,128)(2,1)S(1)} %slice.27), channel_id=1, source_target_pairs={{0,96},{16,112},{32,0},{48,16},{64,32},{80,48},{96,64},{112,80},{1... | collective-permute-start | bytes 1277960 | tf_op jit(solution)/shard_map/ppermute | solution.py:427
  93.1 4.6 %all-to-all-done.4 = bf16[16,8,3328]{2,1,0:T(8,128)(2,1)} async-done(((bf16[16,8,3328]{2,1,0:T(8,128)(2,1)}), bf16[16,8,3328]{2,1,0:T(8,128)(2,1)}, u32[]{:S(2)}, u32[]{:S(2)}) %all-to-all-start.4) | async-done | bytes 852000 | tf_op jit(solution)/shard_map/all_to_all | solution.py:437
  97.6 2.4 %collective-permute-start.12 = (bf16[128,3328]{1,0:T(8,128)(2,1)}, bf16[128,3328]{1,0:T(8,128)(2,1)}, u32[]{:S(2)}, u32[]{:S(2)}) collective-permute-start(bf16[128,3328]{1,0:T(8,128)(2,1)} %bitcast.9.refs_2_), channel_id=1, source_target_pairs={{0,16},{16,0},{32,48},{48,32},{64,80},{80,64},{96,112},{112,96},{1... | collective-permute-start | bytes 2555912 | tf_op jit(solution)/shard_map/ppermute | solution.py:433
  102.7 9.5 %collective-permute-done.2.refs_5_ = bf16[128,3328]{1,0:T(8,128)(2,1)} collective-permute-done((bf16[128,3328]{1,0:T(8,128)(2,1)}, bf16[128,3328]{1,0:T(8,128)(2,1)}, u32[]{:S(2)}, u32[]{:S(2)}) %collective-permute-start.2) | collective-permute-done | bytes 852000 | tf_op jit(solution)/shard_map/ppermute | solution.py:427
  112.8 1.8 slice.30
  114.6 24.9 %collective-permute-done.4.refs_7_ = bf16[64,3328]{1,0:T(8,128)(2,1)S(1)} collective-permute-done((bf16[64,3328]{1,0:T(8,128)(2,1)S(1)}, bf16[64,3328]{1,0:T(8,128)(2,1)S(1)}, u32[]{:S(2)}, u32[]{:S(2)}) %collective-permute-start.4) | collective-permute-done | bytes 426016 | tf_op jit(solution)/shard_map/ppermute | solution.py:427
  139.9 1.5 collective-permute-start.13
  142.8 12.1 %shard_map.57.before_ref = bf16[8,128,1024]{2,1,0:T(8,128)(2,1)} custom-call(s32[3]{0:T(128)} %pad_add_fusion.refs_0_.place_ref, bf16[3328,1024]{1,0:T(8,128)(2,1)} %shard_map.55.refs_1_.weight_ref, bf16[128,3328]{1,0:T(8,128)(2,1)} %bitcast.29, bf16[128,3328]{1,0:T(8,128)(2,1)} %collective-permute-done.refs_3_, ...), custom_call_target="tpu_custom_call" | custom-call | flops 152672665600 | bytes 14614528 | tf_op jit(solution)/shard_map/pallas_call | solution.py:199
  155.0 4.6 %shard_map.58 = bf16[8,128,1024]{2,1,0:T(8,128)(2,1)} custom-call(s32[3]{0:T(128)} %pad_add_fusion.refs_0_.place_ref, bf16[3328,1024]{1,0:T(8,128)(2,1)} %shard_map.55.refs_1_.weight_ref, bf16[8,128,1024]{2,1,0:T(8,128)(2,1)} %shard_map.57.before_ref, bf16[64,3328]{1,0:T(8,128)(2,1)} %copy-done.3, ...), custom_call_target="tpu_custom_call", output_to_operand_aliasing={{}: (2, {})} | custom-call | flops 872415232 | bytes 7929856 | tf_op jit(solution)/shard_map/pallas_call | solution.py:252
  159.6 8.8 %all-to-all-start.2 = ((bf16[16,64,1024]{2,1,0:T(8,128)(2,1)}), bf16[16,64,1024]{2,1,0:T(8,128)(2,1)}, u32[]{:S(2)}, u32[]{:S(2)}) async-start(bf16[16,64,1024]{2,1,0:T(8,128)(2,1)} %bitcast.22), calls=%async_computation.2 | async-start | bytes 4194304 | tf_op jit(solution)/shard_map/all_to_all | solution.py:437
  168.4 8.0 %collective-permute-done.14.refs_8_ = bf16[128,3328]{1,0:T(8,128)(2,1)} collective-permute-done((bf16[128,3328]{1,0:T(8,128)(2,1)}, bf16[128,3328]{1,0:T(8,128)(2,1)}, u32[]{:S(2)}, u32[]{:S(2)}) %collective-permute-start.14) | collective-permute-done | bytes 852000 | tf_op jit(solution)/shard_map/ppermute | solution.py:427
  176.4 1.5 collective-permute-start.15
  177.9 12.3 %shard_map.60 = (f32[8,64,1024]{2,1,0:T(8,128)}, bf16[8,64,1024]{2,1,0:T(8,128)(2,1)}) custom-call(s32[3]{0:T(128)} %pad_add_fusion.refs_0_.place_ref, bf16[3328,1024]{1,0:T(8,128)(2,1)} %shard_map.55.refs_1_.weight_ref, bf16[128,3328]{1,0:T(8,128)(2,1)} %bitcast.9.refs_2_, bf16[128,3328]{1,0:T(8,128)(2,1)} %collective-permute-done.9.refs_3_, ...), custom_call_target="tpu_custom_call" | custom-call | flops 152672665600 | bytes 14614528 | tf_op jit(solution)/shard_map/pallas_call | solution.py:317
  190.2 3.9 %collective-permute-done.15.low_ref.high_ref = bf16[128,3328]{1,0:T(8,128)(2,1)} collective-permute-done((bf16[128,3328]{1,0:T(8,128)(2,1)}, bf16[128,3328]{1,0:T(8,128)(2,1)}, u32[]{:S(2)}, u32[]{:S(2)}) %collective-permute-start.15) | collective-permute-done | bytes 852000 | tf_op jit(solution)/shard_map/ppermute | solution.py:427
  194.2 4.7 %shard_map.61 = (f32[8,64,1024]{2,1,0:T(8,128)}, bf16[8,64,1024]{2,1,0:T(8,128)(2,1)}) custom-call(s32[3]{0:T(128)} %pad_add_fusion.refs_0_.place_ref, bf16[3328,1024]{1,0:T(8,128)(2,1)} %shard_map.55.refs_1_.weight_ref, f32[8,64,1024]{2,1,0:T(8,128)} %get-tuple-element.19.kept, ...), custom_call_target="tpu_custom_call", output_to_operand_aliasing={{0}: (2, {}), {1}: (3, {})} | custom-call | flops 872415232 | bytes 7929856 | tf_op jit(solution)/shard_map/pallas_call | solution.py:383
  198.9 4.0 %collective-permute-start.16 = (bf16[8,64,1024]{2,1,0:T(8,128)(2,1)}, bf16[8,64,1024]{2,1,0:T(8,128)(2,1)S(1)}, u32[]{:S(2)}, u32[]{:S(2)}) collective-permute-start(bf16[8,64,1024]{2,1,0:T(8,128)(2,1)} %get-tuple-element.22), channel_id=1, source_target_pairs={{0,1},{1,0},{2,3},{3,2},{4,5},{5,4},{6,7},{7,6},{8,9},{9,8},{10,11... | collective-permute-start | bytes 3145736 | tf_op jit(solution)/shard_map/ppermute | solution.py:417
  202.9 2.5 %collective-permute-done.16 = bf16[8,64,1024]{2,1,0:T(8,128)(2,1)S(1)} collective-permute-done((bf16[8,64,1024]{2,1,0:T(8,128)(2,1)}, bf16[8,64,1024]{2,1,0:T(8,128)(2,1)S(1)}, u32[]{:S(2)}, u32[]{:S(2)}) %collective-permute-start.16) | collective-permute-done | bytes 1048608 | tf_op jit(solution)/shard_map/ppermute | solution.py:417
  205.4 3.0 %add_convert_fusion = bf16[8,64,1024]{2,1,0:T(8,128)(2,1)} fusion(f32[8,64,1024]{2,1,0:T(8,128)} %get-tuple-element.21, bf16[8,64,1024]{2,1,0:T(8,128)(2,1)S(1)} %collective-permute-done.16), kind=kLoop, calls=%fused_computation.2 | loop fusion | flops 1572864 | bytes 4194304 | tf_op jit(solution)/shard_map/convert_element_type | solution.py:418
  208.3 3.6 %all-to-all-start.5 = ((bf16[8,64,1024]{2,1,0:T(8,128)(2,1)}), bf16[8,64,1024]{2,1,0:T(8,128)(2,1)S(1)}, u32[]{:S(2)}, u32[]{:S(2)}) async-start(bf16[8,64,1024]{2,1,0:T(8,128)(2,1)} %add_convert_fusion), calls=%async_computation.5 | async-start | bytes 2097152 | tf_op jit(solution)/shard_map/all_to_all | solution.py:420
  212.0 2.0 convert_reduce_fusion
  214.0 12.9 %all-to-all-done.5 = bf16[8,64,1024]{2,1,0:T(8,128)(2,1)S(1)} async-done(((bf16[8,64,1024]{2,1,0:T(8,128)(2,1)}), bf16[8,64,1024]{2,1,0:T(8,128)(2,1)S(1)}, u32[]{:S(2)}, u32[]{:S(2)}) %all-to-all-start.5) | async-done | bytes 1048608 | tf_op jit(solution)/shard_map/all_to_all | solution.py:420
  (46 shorter events, 14.1 us)
Async XLA Ops:
  3.5 22.0 %all-to-all-start = ((bf16[16,8,3328]{2,1,0:T(8,128)(2,1)}), bf16[16,8,3328]{2,1,0:T(8,128)(2,1)S(1)}, u32[]{:S(2)}, u32[]{:S(2)}) async-start(bf16[16,8,3328]{2,1,0:T(8,128)(2,1)} %get-tuple-element.24), calls=%async_computation | async-start | bytes 1703936 | tf_op jit(solution)/shard_map/all_to_all | solution.py:437
  25.6 1.0 copy-start.1
  51.7 25.3 %copy-start.2 = (bf16[16,8,3328]{2,1,0:T(8,128)(2,1)}, bf16[16,8,3328]{2,1,0:T(8,128)(2,1)S(1)}, u32[]{:S(2)}) copy-start(bf16[16,8,3328]{2,1,0:T(8,128)(2,1)S(1)} %all_to_all.30) | copy-start | bytes 2555908
  51.8 18.3 %all-to-all-start.3 = ((bf16[16,8,3328]{2,1,0:T(8,128)(2,1)}), bf16[16,8,3328]{2,1,0:T(8,128)(2,1)S(1)}, u32[]{:S(2)}, u32[]{:S(2)}) async-start(bf16[16,8,3328]{2,1,0:T(8,128)(2,1)} %get-tuple-element.18), calls=%async_computation.3 | async-start | bytes 1703936 | tf_op jit(solution)/shard_map/all_to_all | solution.py:437
  56.3 31.2 %collective-permute-start.3 = (bf16[128,3328]{1,0:T(8,128)(2,1)S(1)}, bf16[128,3328]{1,0:T(8,128)(2,1)S(1)}, u32[]{:S(2)}, u32[]{:S(2)}) collective-permute-start(bf16[128,3328]{1,0:T(8,128)(2,1)S(1)} %bitcast.26), channel_id=1, source_target_pairs={{0,16},{16,0},{32,48},{48,32},{64,80},{80,64},{96,112},{112,96},{1... | collective-permute-start | bytes 2555912 | tf_op jit(solution)/shard_map/ppermute | solution.py:433
  58.8 31.6 %collective-permute-start = (bf16[128,3328]{1,0:T(8,128)(2,1)S(1)}, bf16[128,3328]{1,0:T(8,128)(2,1)}, u32[]{:S(2)}, u32[]{:S(2)}) collective-permute-start(bf16[128,3328]{1,0:T(8,128)(2,1)S(1)} %bitcast.27), channel_id=1, source_target_pairs={{0,32},{16,48},{32,64},{48,80},{64,96},{80,112},{96,0},{112,16},{1... | collective-permute-start | bytes 2555912 | tf_op jit(solution)/shard_map/ppermute | solution.py:427
  60.1 31.4 %collective-permute-start.1 = (bf16[128,3328]{1,0:T(8,128)(2,1)S(1)}, bf16[128,3328]{1,0:T(8,128)(2,1)}, u32[]{:S(2)}, u32[]{:S(2)}) collective-permute-start(bf16[128,3328]{1,0:T(8,128)(2,1)S(1)} %bitcast.28), channel_id=1, source_target_pairs={{0,96},{16,112},{32,0},{48,16},{64,32},{80,48},{96,64},{112,80},{1... | collective-permute-start | bytes 2555912 | tf_op jit(solution)/shard_map/ppermute | solution.py:427
  70.1 0.9 copy-start
  77.1 20.5 %all-to-all-start.4 = ((bf16[16,8,3328]{2,1,0:T(8,128)(2,1)}), bf16[16,8,3328]{2,1,0:T(8,128)(2,1)}, u32[]{:S(2)}, u32[]{:S(2)}) async-start(bf16[16,8,3328]{2,1,0:T(8,128)(2,1)} %shard_map.59), calls=%async_computation.4 | async-start | bytes 1703936 | tf_op jit(solution)/shard_map/all_to_all | solution.py:437
  87.5 5.1 %copy-start.4 = (bf16[128,3328]{1,0:T(8,128)(2,1)}, bf16[128,3328]{1,0:T(8,128)(2,1)S(1)}, u32[]{:S(2)}) copy-start(bf16[128,3328]{1,0:T(8,128)(2,1)S(1)} %collective-permute-done.3.refs_6_) | copy-start | bytes 2555908
  87.5 13.9 %collective-permute-start.5 = (bf16[64,3328]{1,0:T(8,128)(2,1)S(1)}, bf16[64,3328]{1,0:T(8,128)(2,1)S(1)}, u32[]{:S(2)}, u32[]{:S(2)}) collective-permute-start(bf16[64,3328]{1,0:T(8,128)(2,1)S(1)} %slice.27), channel_id=1, source_target_pairs={{0,96},{16,112},{32,0},{48,16},{64,32},{80,48},{96,64},{112,80},{1... | collective-permute-start | bytes 1277960 | tf_op jit(solution)/shard_map/ppermute | solution.py:427
  91.4 20.9 %collective-permute-start.2 = (bf16[128,3328]{1,0:T(8,128)(2,1)}, bf16[128,3328]{1,0:T(8,128)(2,1)}, u32[]{:S(2)}, u32[]{:S(2)}) collective-permute-start(bf16[128,3328]{1,0:T(8,128)(2,1)} %collective-permute-done.refs_3_), channel_id=1, source_target_pairs={{0,32},{16,48},{32,64},{48,80},{64,96},{80,112},{96,0},{112,16},{1... | collective-permute-start | bytes 2555912 | tf_op jit(solution)/shard_map/ppermute | solution.py:427
  92.6 46.9 %collective-permute-start.6 = (bf16[128,3328]{1,0:T(8,128)(2,1)S(1)}, bf16[128,3328]{1,0:T(8,128)(2,1)}, u32[]{:S(2)}, u32[]{:S(2)}) collective-permute-start(bf16[128,3328]{1,0:T(8,128)(2,1)S(1)} %pad_maximum_fusion), channel_id=1, source_target_pairs={{0,16},{16,0},{32,48},{48,32},{64,80},{80,64},{96,112},{112,96},{1... | collective-permute-start | bytes 2555912 | tf_op jit(solution)/shard_map/ppermute | solution.py:433
  97.6 42.3 %collective-permute-start.12 = (bf16[128,3328]{1,0:T(8,128)(2,1)}, bf16[128,3328]{1,0:T(8,128)(2,1)}, u32[]{:S(2)}, u32[]{:S(2)}) collective-permute-start(bf16[128,3328]{1,0:T(8,128)(2,1)} %bitcast.9.refs_2_), channel_id=1, source_target_pairs={{0,16},{16,0},{32,48},{48,32},{64,80},{80,64},{96,112},{112,96},{1... | collective-permute-start | bytes 2555912 | tf_op jit(solution)/shard_map/ppermute | solution.py:433
  100.1 41.3 %collective-permute-start.9 = (bf16[128,3328]{1,0:T(8,128)(2,1)}, bf16[128,3328]{1,0:T(8,128)(2,1)}, u32[]{:S(2)}, u32[]{:S(2)}) collective-permute-start(bf16[128,3328]{1,0:T(8,128)(2,1)} %bitcast.9.refs_2_), channel_id=1, source_target_pairs={{0,32},{16,48},{32,64},{48,80},{64,96},{80,112},{96,0},{112,16},{1... | collective-permute-start | bytes 2555912 | tf_op jit(solution)/shard_map/ppermute | solution.py:427
  101.4 41.4 %copy-start.5 = (bf16[64,3328]{1,0:T(8,128)(2,1)}, bf16[64,3328]{1,0:T(8,128)(2,1)S(1)}, u32[]{:S(2)}) copy-start(bf16[64,3328]{1,0:T(8,128)(2,1)S(1)} %collective-permute-done.5.refs_8_) | copy-start | bytes 1277956
  101.4 38.1 %collective-permute-start.4 = (bf16[64,3328]{1,0:T(8,128)(2,1)S(1)}, bf16[64,3328]{1,0:T(8,128)(2,1)S(1)}, u32[]{:S(2)}, u32[]{:S(2)}) collective-permute-start(bf16[64,3328]{1,0:T(8,128)(2,1)S(1)} %slice.27), channel_id=1, source_target_pairs={{0,32},{16,48},{32,64},{48,80},{64,96},{80,112},{96,0},{112,16},{1... | collective-permute-start | bytes 1277960 | tf_op jit(solution)/shard_map/ppermute | solution.py:427
  112.2 27.7 %collective-permute-start.7 = (bf16[64,3328]{1,0:T(8,128)(2,1)S(1)}, bf16[64,3328]{1,0:T(8,128)(2,1)S(1)}, u32[]{:S(2)}, u32[]{:S(2)}) collective-permute-start(bf16[64,3328]{1,0:T(8,128)(2,1)S(1)} %collective-permute-done.5.refs_8_), channel_id=1, source_target_pairs={{0,96},{16,112},{32,0},{48,16},{64,32},{80,48},{96,64},{112,80},{1... | collective-permute-start | bytes 1277960 | tf_op jit(solution)/shard_map/ppermute | solution.py:427
  139.5 3.3 %copy-start.6 = (bf16[64,3328]{1,0:T(8,128)(2,1)}, bf16[64,3328]{1,0:T(8,128)(2,1)S(1)}, u32[]{:S(2)}) copy-start(bf16[64,3328]{1,0:T(8,128)(2,1)S(1)} %collective-permute-done.4.refs_7_) | copy-start | bytes 1277956
  139.5 38.4 %collective-permute-start.10 = (bf16[128,3328]{1,0:T(8,128)(2,1)}, bf16[128,3328]{1,0:T(8,128)(2,1)}, u32[]{:S(2)}, u32[]{:S(2)}) collective-permute-start(bf16[128,3328]{1,0:T(8,128)(2,1)} %bitcast.9.refs_2_), channel_id=1, source_target_pairs={{0,96},{16,112},{32,0},{48,16},{64,32},{80,48},{96,64},{112,80},{1... | collective-permute-start | bytes 2555912 | tf_op jit(solution)/shard_map/ppermute | solution.py:427
  139.5 15.4 %collective-permute-start.8 = (bf16[64,3328]{1,0:T(8,128)(2,1)}, bf16[64,3328]{1,0:T(8,128)(2,1)}, u32[]{:S(2)}, u32[]{:S(2)}) collective-permute-start(bf16[64,3328]{1,0:T(8,128)(2,1)} %slice.30), channel_id=1, source_target_pairs={{0,16},{16,0},{32,48},{48,32},{64,80},{80,64},{96,112},{112,96},{1... | collective-permute-start | bytes 1277960 | tf_op jit(solution)/shard_map/ppermute | solution.py:433
  139.9 36.5 %collective-permute-start.14 = (bf16[128,3328]{1,0:T(8,128)(2,1)}, bf16[128,3328]{1,0:T(8,128)(2,1)}, u32[]{:S(2)}, u32[]{:S(2)}) collective-permute-start(bf16[128,3328]{1,0:T(8,128)(2,1)} %collective-permute-done.12.refs_6_), channel_id=1, source_target_pairs={{0,96},{16,112},{32,0},{48,16},{64,32},{80,48},{96,64},{112,80},{1... | collective-permute-start | bytes 2555912 | tf_op jit(solution)/shard_map/ppermute | solution.py:427
  139.9 15.0 %copy-start.3 = (bf16[64,3328]{1,0:T(8,128)(2,1)}, bf16[64,3328]{1,0:T(8,128)(2,1)S(1)}, u32[]{:S(2)}) copy-start(bf16[64,3328]{1,0:T(8,128)(2,1)S(1)} %collective-permute-done.7.low_ref) | copy-start | bytes 1277956
  139.9 38.0 %collective-permute-start.13 = (bf16[128,3328]{1,0:T(8,128)(2,1)}, bf16[128,3328]{1,0:T(8,128)(2,1)}, u32[]{:S(2)}, u32[]{:S(2)}) collective-permute-start(bf16[128,3328]{1,0:T(8,128)(2,1)} %collective-permute-done.12.refs_6_), channel_id=1, source_target_pairs={{0,32},{16,48},{32,64},{48,80},{64,96},{80,112},{96,0},{112,16},{1... | collective-permute-start | bytes 2555912 | tf_op jit(solution)/shard_map/ppermute | solution.py:427
  141.4 36.5 %collective-permute-start.11 = (bf16[128,3328]{1,0:T(8,128)(2,1)}, bf16[128,3328]{1,0:T(8,128)(2,1)}, u32[]{:S(2)}, u32[]{:S(2)}) collective-permute-start(bf16[128,3328]{1,0:T(8,128)(2,1)} %collective-permute-done.9.refs_3_), channel_id=1, source_target_pairs={{0,32},{16,48},{32,64},{48,80},{64,96},{80,112},{96,0},{112,16},{1... | collective-permute-start | bytes 2555912 | tf_op jit(solution)/shard_map/ppermute | solution.py:427
  159.6 48.7 %all-to-all-start.2 = ((bf16[16,64,1024]{2,1,0:T(8,128)(2,1)}), bf16[16,64,1024]{2,1,0:T(8,128)(2,1)}, u32[]{:S(2)}, u32[]{:S(2)}) async-start(bf16[16,64,1024]{2,1,0:T(8,128)(2,1)} %bitcast.22), calls=%async_computation.2 | async-start | bytes 4194304 | tf_op jit(solution)/shard_map/all_to_all | solution.py:437
  176.4 17.7 %collective-permute-start.15 = (bf16[128,3328]{1,0:T(8,128)(2,1)}, bf16[128,3328]{1,0:T(8,128)(2,1)}, u32[]{:S(2)}, u32[]{:S(2)}) collective-permute-start(bf16[128,3328]{1,0:T(8,128)(2,1)} %collective-permute-done.14.refs_8_), channel_id=1, source_target_pairs={{0,96},{16,112},{32,0},{48,16},{64,32},{80,48},{96,64},{112,80},{1... | collective-permute-start | bytes 2555912 | tf_op jit(solution)/shard_map/ppermute | solution.py:427
  198.9 6.5 %collective-permute-start.16 = (bf16[8,64,1024]{2,1,0:T(8,128)(2,1)}, bf16[8,64,1024]{2,1,0:T(8,128)(2,1)S(1)}, u32[]{:S(2)}, u32[]{:S(2)}) collective-permute-start(bf16[8,64,1024]{2,1,0:T(8,128)(2,1)} %get-tuple-element.22), channel_id=1, source_target_pairs={{0,1},{1,0},{2,3},{3,2},{4,5},{5,4},{6,7},{7,6},{8,9},{9,8},{10,11... | collective-permute-start | bytes 3145736 | tf_op jit(solution)/shard_map/ppermute | solution.py:417
  208.3 18.6 %all-to-all-start.5 = ((bf16[8,64,1024]{2,1,0:T(8,128)(2,1)}), bf16[8,64,1024]{2,1,0:T(8,128)(2,1)S(1)}, u32[]{:S(2)}, u32[]{:S(2)}) async-start(bf16[8,64,1024]{2,1,0:T(8,128)(2,1)} %add_convert_fusion), calls=%async_computation.5 | async-start | bytes 2097152 | tf_op jit(solution)/shard_map/all_to_all | solution.py:420
